TPU v7x, 32 devices: a whole 2x2x4 slice. The times are simulated.
32 devices in a mesh: item: 8 (over z, x), day: 4 (over y, core).
Axes of the slice: x: 2, y: 2, z: 4, core: 2. Of those that a mesh axis runs over, the one named last changes fastest.
Arguments:
- user_factors: float32 [256, 512], P(('item', 'day')), may hold values from 0.005 to 0.012
- item_factors: bfloat16 [4096, 512], P('item'), may hold values from 0 to 1
- day_factors: bfloat16 [184, 512], P('day'), may hold values from 0.099609375 to 1
- tile_counts: bfloat16 [4096, 128, 128], P(('item', 'day')), may hold values from 0 to 2
- tile_index: int32 [3, 4096], P(None, ('item', 'day')), may hold values from 0 to 45, as said below
- tile_live: int32 [32], P(('item', 'day')), may hold values from 32 to 128, as said below
Outputs:
- updated_users: float32 [256, 512], P(('item', 'day'))
Inputs may be any that keep to these rules, and one draw needn't show every extreme that they name: `tile_index`: row 0 names a user block below 2, row 1 an item block below 4 and row 2 a day below 46, local to the device that holds the slot. Only the first tile_live[d] slots of list d are live; some list has all 128 live.
All inputs are finite; a program needn't handle non-finite values.
Results may differ from a plain program's by a relative error of at most 0.003.
Values may be sent and summed in bfloat16 or wider, within the bound.
No kernel may reach another device: no remote copies, remote signals or barrier semaphores. Data moves between devices by JAX's collectives and lax.ppermute only.
A program may use at most 64 MiB of HBM per device.

v0:
```python
import jax
import jax.numpy as jnp
from jax import lax
from jax.experimental import pallas as pl
from jax.experimental.pallas import tpu as pltpu
from jax.sharding import PartitionSpec as P

TILE = 128
GROUP = 4
UNROLL = 4
CHUNK = 16
LANES = 128
NEEDS = 8
VMEM = pl.BlockSpec(memory_space=pltpu.VMEM)
SMEM = pl.BlockSpec(memory_space=pltpu.SMEM)
HBM = pl.BlockSpec(memory_space=pltpu.HBM)
MIB = 1024 * 1024


def round_up(n, m):
    return (n + m - 1) // m * m


def plan_kernel(
    index_far, live_far, days_far, mate_index_far, mate_live_far, mate_days_far, items_far,
    plan, items, day_rows, extra,
    index, live, days, mate_index, mate_live, mate_days, spots, sems,
):
    rank = items.shape[1]
    fetch = [
        pltpu.make_async_copy(far, near, sems.at[i])
        for i, (far, near) in enumerate(
            (
                (index_far, index),
                (live_far, live),
                (mate_index_far, mate_index),
                (mate_live_far, mate_live),
                (days_far, days),
                (mate_days_far, mate_days),
                (items_far, items),
            )
        )
    ]
    for copy in fetch:
        copy.start()

    def clear(i, carry):
        for j in range(LANES):
            plan[i, j] = -1
        return carry

    lax.fori_loop(1, plan.shape[0], clear, 0)
    for j in range(LANES):
        plan[0, j] = 0
    for u in range(spots.shape[0]):
        spots[u] = 0
    for copy in fetch[:4]:
        copy.wait()

    mine, other = live[0], mate_live[0]
    half = (mine + other + 1) >> 1
    keep, mate_keep = jnp.minimum(mine, half), jnp.minimum(other, half)
    parts = jnp.maximum((keep + CHUNK - 1) // CHUNK, 2)
    mate_first = mate_keep // CHUNK
    mate_parts = jnp.where(mate_keep < other, (other + CHUNK - 1) // CHUNK - mate_first, 0)
    plan[0, 1] = parts
    plan[0, 2] = mate_first
    plan[0, 3] = parts + mate_parts

    def enlist(table, low, high, shift, day_shift, used):
        def place(u, code, tile, used):
            spot = spots[u]
            new = (spot & (GROUP - 1)) == 0
            spot = jnp.where(new, used * GROUP, spot)
            spots[u] = spot + 1
            plan[1 + (spot >> 7), spot & (LANES - 1)] = code
            plan[0, NEEDS + spot // (GROUP * UNROLL)] = (tile >> 4) + 1
            return used + new.astype(jnp.int32)

        def read(s):
            u, tile = table[0, s], s + shift
            code = (u << 24) | (tile << 16) | (table[1, s] << 8) | (table[2, s] + day_shift)
            return u, code, tile

        def four(t, used):
            found = [read(low + t * 4 + j) for j in range(4)]
            for u, code, tile in found:
                used = place(u, code, tile, used)
            return used

        def one(s, used):
            return place(*read(s), used)

        fours = (high - low) >> 2
        used = lax.fori_loop(0, fours, four, used)
        return lax.fori_loop(low + fours * 4, high, one, used)

    used = enlist(index, 0, keep, 0, 0, jnp.int32(0))
    used = enlist(
        mate_index, mate_keep, other, (parts - mate_first) * CHUNK, day_rows.shape[0] // 2, used
    )
    plan[0, 0] = (used + UNROLL - 1) // UNROLL

    for copy in fetch[4:]:
        copy.wait()
    count = days.shape[0]
    day_rows[0:count, :] = days[...].astype(jnp.float32)
    day_rows[day_rows.shape[0] // 2 : day_rows.shape[0] // 2 + count, :] = mate_days[...].astype(
        jnp.float32
    )
    day_sum = jnp.sum(days[...].astype(jnp.float32), axis=0, keepdims=True)
    item_sum = jnp.sum(items[...].astype(jnp.float32), axis=0, keepdims=True)
    item_at, day_at = lax.axis_index("item"), lax.axis_index("day")
    row = lax.broadcasted_iota(jnp.int32, (8, LANES), 0)
    block = jnp.zeros((8, LANES), jnp.float32)
    for q in range(rank // LANES):
        for first, total, at in ((0, item_sum, day_at), (2, day_sum, item_at)):
            part = jnp.where(at == q, total[:, q * LANES : (q + 1) * LANES], 0.0)
            high = part.astype(jnp.bfloat16).astype(jnp.float32)
            block = jnp.where(row == first, block + high, block)
            block = jnp.where(row == first + 1, block + (part - high), block)
    extra[...] = block


def tiles_kernel(
    plan_far, counts_far, mate_counts_far, users, items, day_rows, extra,
    out,
    plan, counts, phi, plan_sem, counts_sem, *buffers,
):
    weighted, ratios = buffers[:UNROLL], buffers[UNROLL:]
    rank = users.shape[1]
    fetch = pltpu.make_async_copy(plan_far, plan, plan_sem)
    fetch.start()

    def part(far, c, at):
        source = far.at[pl.ds(pl.multiple_of(c * CHUNK, CHUNK), CHUNK)]
        target = counts.at[pl.ds(pl.multiple_of(at * CHUNK, CHUNK), CHUNK)]
        return pltpu.make_async_copy(source, target, counts_sem.at[at])

    part(counts_far, 0, 0).start()
    part(counts_far, 1, 1).start()
    phi[...] = jnp.zeros_like(phi)
    weighted[-1][...] = jnp.zeros_like(weighted[-1])
    ratios[-1][...] = jnp.zeros_like(ratios[-1])
    fetch.wait()
    turns, parts, mate_first, all_parts = plan[0, 0], plan[0, 1], plan[0, 2], plan[0, 3]

    def start_part(c, carry):
        part(counts_far, c, c).start()
        return carry

    def start_mate_part(c, carry):
        part(mate_counts_far, mate_first + c - parts, c).start()
        return carry

    def wait_part(c, carry):
        part(counts_far, 0, c).wait()
        return carry

    lax.fori_loop(2, parts, start_part, 0)
    lax.fori_loop(parts, all_parts, start_mate_part, 0)
    out[:, :, rank:] = jnp.broadcast_to(
        extra[...].astype(jnp.bfloat16)[None], (out.shape[0], 8, LANES)
    )

    def code_at(spot):
        return plan[1 + (spot >> 7), spot & (LANES - 1)]

    def block_of(g):
        return pl.ds(pl.multiple_of((jnp.maximum(code_at(g * GROUP), 0) >> 24) * TILE, TILE), TILE)

    def make_ratio(g, i):
        rows = users[block_of(g), :]
        codes = [code_at(g * GROUP + j) for j in range(GROUP)]
        slots = [jnp.maximum(code, 0) for code in codes]
        for j, slot in enumerate(slots):
            item = pl.multiple_of(((slot >> 8) & 255) * TILE, TILE)
            scale = day_rows[pl.ds(slot & 255, 1), :].astype(jnp.bfloat16)
            weighted[i][j * TILE : (j + 1) * TILE, :] = items[pl.ds(item, TILE), :] * scale
        model = lax.dot_general(
            rows, weighted[i][...], (((1,), (1,)), ((), ())), preferred_element_type=jnp.float32
        )
        for j, slot in enumerate(slots):
            cols = slice(j * TILE, (j + 1) * TILE)
            ratio = counts[(slot >> 16) & 255].astype(jnp.float32) / model[:, cols]
            ratios[i][:, cols] = jnp.where(codes[j] >= 0, ratio, 0.0).astype(jnp.bfloat16)

    def add_terms(g, i):
        phi[block_of(g), :] += jnp.dot(
            ratios[i][...], weighted[i][...], preferred_element_type=jnp.float32
        )

    def turn(t, ready):
        need = jnp.maximum(plan[0, NEEDS + t], ready)
        lax.fori_loop(ready, need, wait_part, 0)
        for i in range(UNROLL):
            g = t * UNROLL + i
            make_ratio(g, i)
            add_terms(jnp.maximum(g - 1, 0), (i - 1) % UNROLL)
        return need

    ready = lax.fori_loop(0, turns, turn, jnp.int32(0))
    lax.fori_loop(ready, all_parts, wait_part, 0)
    add_terms(jnp.maximum(turns * UNROLL - 1, 0), UNROLL - 1)
    out[:, :, 0:rank] = phi[...].reshape(out.shape[0], out.shape[1], rank).astype(jnp.bfloat16)


def finish_kernel(n_item, n_day, received, user_factors, out):
    rank = user_factors.shape[1]
    phi = jnp.sum(received[:, :, 0:rank].astype(jnp.float32), axis=0)
    for q in range(rank // LANES):
        cols = slice(q * LANES, (q + 1) * LANES)
        item = received[q, :, rank:].astype(jnp.float32)
        for i in range(1, n_item):
            item = item + received[i * n_day + q, :, rank:].astype(jnp.float32)
        day = received[q * n_day, :, rank:].astype(jnp.float32)
        for k in range(1, n_day):
            day = day + received[q * n_day + k, :, rank:].astype(jnp.float32)
        totals = (item[0:1] + item[1:2]) * (day[2:3] + day[3:4])
        out[:, cols] = user_factors[:, cols] * phi[:, cols] / totals


def solution(mesh):
    n_item, n_day = mesh.shape["item"], mesh.shape["day"]
    devices = n_item * n_day
    axes = ("item", "day")
    mates = [(k, k ^ 1) for k in range(n_day)]

    def per_device(user_factors, item_factors, day_factors, tile_counts, tile_index, tile_live):
        own, rank = user_factors.shape
        blocks = own * devices // TILE
        cap = tile_counts.shape[0]
        day_space = round_up(day_factors.shape[0], 8)
        groups = round_up(cap // GROUP + blocks, UNROLL)
        plan_shape = (1 + pl.cdiv(groups * GROUP, LANES), LANES)
        mate_counts, mate_index, mate_live, mate_days = (
            lax.ppermute(x, "day", mates)
            for x in (tile_counts, tile_index, tile_live, day_factors)
        )
        spread = jnp.broadcast_to(user_factors.astype(jnp.bfloat16)[None], (devices, own, rank))
        gathered = lax.all_to_all(spread, axes, 0, 0, tiled=True).reshape(devices * own, rank)
        plan, items, day_rows, extra = pl.pallas_call(
            plan_kernel,
            out_shape=(
                jax.ShapeDtypeStruct(plan_shape, jnp.int32),
                jax.ShapeDtypeStruct(item_factors.shape, jnp.bfloat16),
                jax.ShapeDtypeStruct((2 * day_space, rank), jnp.float32),
                jax.ShapeDtypeStruct((8, LANES), jnp.float32),
            ),
            in_specs=[HBM] * 7,
            out_specs=(SMEM, VMEM, VMEM, VMEM),
            scratch_shapes=[
                pltpu.SMEM(tile_index.shape, jnp.int32),
                pltpu.SMEM(tile_live.shape, jnp.int32),
                pltpu.VMEM(day_factors.shape, jnp.bfloat16),
                pltpu.SMEM(tile_index.shape, jnp.int32),
                pltpu.SMEM(tile_live.shape, jnp.int32),
                pltpu.VMEM(day_factors.shape, jnp.bfloat16),
                pltpu.SMEM((blocks,), jnp.int32),
                pltpu.SemaphoreType.DMA((7,)),
            ],
            compiler_params=pltpu.CompilerParams(vmem_limit_bytes=16 * MIB),
        )(tile_index, tile_live, day_factors, mate_index, mate_live, mate_days, item_factors)
        partial = pl.pallas_call(
            tiles_kernel,
            out_shape=jax.ShapeDtypeStruct((devices, own, rank + LANES), jnp.bfloat16),
            in_specs=[HBM, HBM, HBM, VMEM, VMEM, VMEM, VMEM],
            out_specs=VMEM,
            scratch_shapes=[
                pltpu.SMEM(plan_shape, jnp.int32),
                pltpu.VMEM((cap + 2 * CHUNK, *tile_counts.shape[1:]), jnp.bfloat16),
                pltpu.VMEM((blocks * TILE, rank), jnp.float32),
                pltpu.SemaphoreType.DMA,
                pltpu.SemaphoreType.DMA((cap // CHUNK + 2,)),
            ]
            + [pltpu.VMEM((GROUP * TILE, rank), jnp.bfloat16)] * UNROLL
            + [pltpu.VMEM((TILE, GROUP * TILE), jnp.bfloat16)] * UNROLL,
            compiler_params=pltpu.CompilerParams(vmem_limit_bytes=51 * MIB),
        )(plan, tile_counts, mate_counts, gathered, items, day_rows, extra)
        received = lax.all_to_all(partial, axes, 0, 0, tiled=True)
        return pl.pallas_call(
            lambda *refs: finish_kernel(n_item, n_day, *refs),
            out_shape=jax.ShapeDtypeStruct((own, rank), jnp.float32),
            in_specs=[VMEM, VMEM],
            out_specs=VMEM,
            compiler_params=pltpu.CompilerParams(vmem_limit_bytes=16 * MIB),
        )(received, user_factors)

    in_specs = (
        P(axes, None),
        P("item", None),
        P("day", None),
        P(axes, None, None),
        P(None, axes),
        P(axes),
    )
    return jax.shard_map(
        per_device, mesh=mesh, in_specs=in_specs, out_specs=P(axes, None), check_vma=False
    )
```

profile of v0, /device:TPU:0, one launch (start us, length us, event | category | flops | bytes accessed | tf_op | source)
XLA Modules:
  0.0 42.0 jit_solution(17183529159150792468)
XLA Ops:
  0.0 0.5 %collective-permute-start.3 = (bf16[128,128,128]{2,1,0:T(8,128)(2,1)}, bf16[128,128,128]{2,1,0:T(8,128)(2,1)}, u32[]{:S(2)}, u32[]{:S(2)}) collective-permute-start(bf16[128,128,128]{2,1,0:T(8,128)(2,1)} %counts_far.1), channel_id=1, source_target_pairs={{0,1},{1,0},{2,3},{3,2},{4,5},{5,4},{6,7},{7,6},{8,9},{9,8},{10,11... | collective-permute-start | bytes 12582920 | tf_op jit(solution)/shard_map/ppermute | solution.py:237
  0.5 0.7 %convert_element_type.3 = bf16[8,512]{1,0:T(8,128)(2,1)S(1)} convert(f32[8,512]{1,0:T(8,128)} %refs_1_.1) | non-fusion elementwise | flops 4096 | bytes 24576 | tf_op jit(solution)/shard_map/convert_element_type | solution.py:240
  1.2 0.7 %broadcast_in_dim.2 = bf16[32,8,512]{2,1,0:T(8,128)(2,1)} broadcast(bf16[8,512]{1,0:T(8,128)(2,1)S(1)} %convert_element_type.3), dimensions={1,2} | broadcast | bytes 270336 | tf_op jit(solution)/shard_map/broadcast_in_dim | solution.py:240
  1.9 7.0 %all-to-all-start = ((bf16[32,8,512]{2,1,0:T(8,128)(2,1)}), bf16[32,8,512]{2,1,0:T(8,128)(2,1)S(1)}, u32[]{:S(2)}, u32[]{:S(2)}) async-start(bf16[32,8,512]{2,1,0:T(8,128)(2,1)} %broadcast_in_dim.2), calls=%async_computation | async-start | bytes 524288 | tf_op jit(solution)/shard_map/all_to_all | solution.py:241
  8.9 0.3 collective-permute-start.2
  9.2 0.3 collective-permute-start
  9.4 0.3 collective-permute-start.1
  10.3 0.3 collective-permute-done.1.mate_live_far
  10.7 0.0 collective-permute-done.mate_index_far
  10.7 0.0 collective-permute-done.2.mate_days_far
  10.7 0.0 copy-start
  10.7 1.0 %copy-done = bf16[512,512]{1,0:T(8,128)(2,1)S(1)} copy-done((bf16[512,512]{1,0:T(8,128)(2,1)S(1)}, bf16[512,512]{1,0:T(8,128)(2,1)}, u32[]{:S(2)}) %copy-start) | copy-done | bytes 524312
  11.7 0.0 copy-start.2
  11.7 0.8 %copy-done.2 = bf16[46,512]{1,0:T(8,128)(2,1)S(1)} copy-done((bf16[46,512]{1,0:T(8,128)(2,1)S(1)}, bf16[46,512]{1,0:T(8,128)(2,1)}, u32[]{:S(2)}) %copy-start.2) | copy-done | bytes 47128
  12.5 0.0 copy-start.3
  12.5 0.7 %copy-done.3 = s32[3,128]{1,0:T(4,128)S(1)} copy-done((s32[3,128]{1,0:T(4,128)S(1)}, s32[3,128]{1,0:T(4,128)}, u32[]{:S(2)}) %copy-start.3) | copy-done | bytes 1560
  13.2 2.8 %shard_map.64 = (s32[3,128]{1,0:T(4,128)S(1)}, bf16[512,512]{1,0:T(8,128)(2,1)S(1)}, f32[96,512]{1,0:T(8,128)S(1)}, f32[8,128]{1,0:T(8,128)S(1)}) custom-call(s32[3,128]{1,0:T(4,128)S(1)} %copy-done.3, s32[1]{0:T(128)S(6)} %copy.7.live_far, bf16[46,512]{1,0:T(8,128)(2,1)S(1)} %copy-done.2, s32[3,128]{1,0:T(4,128)S(1)} %collective-permute-done.mate_index_far, ...), custom_call_target="tpu_custom_call" | custom-call | tf_op jit(solution)/shard_map/pallas_call | solution.py:242
  16.0 3.5 %all-to-all-done = bf16[32,8,512]{2,1,0:T(8,128)(2,1)S(1)} async-done(((bf16[32,8,512]{2,1,0:T(8,128)(2,1)}), bf16[32,8,512]{2,1,0:T(8,128)(2,1)S(1)}, u32[]{:S(2)}, u32[]{:S(2)}) %all-to-all-start) | async-done | bytes 262176 | tf_op jit(solution)/shard_map/all_to_all | solution.py:241
  19.5 0.0 collective-permute-done.3.mate_counts_far
  19.5 0.0 copy-start.1
  19.5 5.2 %shard_map.65 = bf16[32,8,640]{2,1,0:T(8,128)(2,1)S(1)} custom-call(s32[3,128]{1,0:T(4,128)S(1)} %get-tuple-element.9.plan_far, bf16[128,128,128]{2,1,0:T(8,128)(2,1)} %counts_far.1, bf16[128,128,128]{2,1,0:T(8,128)(2,1)} %collective-permute-done.3.mate_counts_far, bf16[256,512]{1,0:T(8,128)(2,1)S(1)} %bitcast.1, ...), custom_call_target="tpu_custom_call" | custom-call | tf_op jit(solution)/shard_map/pallas_call | solution.py:264
  24.6 16.7 %all_to_all.10.refs_0_ = bf16[32,8,640]{2,1,0:T(8,128)(2,1)S(1)} all-to-all(bf16[32,8,640]{2,1,0:T(8,128)(2,1)S(1)} %shard_map.65), channel_id=1, replica_groups=mesh['item'=8,'day'=4] {'item','day'}, dimensions={0} | all-to-all | bytes 655360 | tf_op jit(solution)/shard_map/all_to_all | solution.py:280
  41.3 0.0 copy-done.1
  41.3 0.7 %shard_map.66 = f32[8,512]{1,0:T(8,128)} custom-call(bf16[32,8,640]{2,1,0:T(8,128)(2,1)S(1)} %all_to_all.10.refs_0_, f32[8,512]{1,0:T(8,128)S(1)} %copy-done.1), custom_call_target="tpu_custom_call" | custom-call | tf_op jit(solution)/shard_map/pallas_call | solution.py:281
Async XLA Ops:
  0.0 19.5 %collective-permute-start.3 = (bf16[128,128,128]{2,1,0:T(8,128)(2,1)}, bf16[128,128,128]{2,1,0:T(8,128)(2,1)}, u32[]{:S(2)}, u32[]{:S(2)}) collective-permute-start(bf16[128,128,128]{2,1,0:T(8,128)(2,1)} %counts_far.1), channel_id=1, source_target_pairs={{0,1},{1,0},{2,3},{3,2},{4,5},{5,4},{6,7},{7,6},{8,9},{9,8},{10,11... | collective-permute-start | bytes 12582920 | tf_op jit(solution)/shard_map/ppermute | solution.py:237
  1.9 17.6 %all-to-all-start = ((bf16[32,8,512]{2,1,0:T(8,128)(2,1)}), bf16[32,8,512]{2,1,0:T(8,128)(2,1)S(1)}, u32[]{:S(2)}, u32[]{:S(2)}) async-start(bf16[32,8,512]{2,1,0:T(8,128)(2,1)} %broadcast_in_dim.2), calls=%async_computation | async-start | bytes 524288 | tf_op jit(solution)/shard_map/all_to_all | solution.py:241
  8.9 1.8 %collective-permute-start.2 = (bf16[46,512]{1,0:T(8,128)(2,1)}, bf16[46,512]{1,0:T(8,128)(2,1)S(1)}, u32[]{:S(2)}, u32[]{:S(2)}) collective-permute-start(bf16[46,512]{1,0:T(8,128)(2,1)} %days_far.1), channel_id=1, source_target_pairs={{0,1},{1,0},{2,3},{3,2},{4,5},{5,4},{6,7},{7,6},{8,9},{9,8},{10,11... | collective-permute-start | bytes 141320 | tf_op jit(solution)/shard_map/ppermute | solution.py:237
  9.2 1.5 %collective-permute-start = (s32[3,128]{1,0:T(4,128)}, s32[3,128]{1,0:T(4,128)S(1)}, u32[]{:S(2)}, u32[]{:S(2)}) collective-permute-start(s32[3,128]{1,0:T(4,128)} %index_far.1), channel_id=1, source_target_pairs={{0,1},{1,0},{2,3},{3,2},{4,5},{5,4},{6,7},{7,6},{8,9},{9,8},{10,11... | collective-permute-start | bytes 4616 | tf_op jit(solution)/shard_map/ppermute | solution.py:237
  9.4 1.2 %collective-permute-start.1 = (s32[1]{0:T(128)}, s32[1]{0:T(128)}, u32[]{:S(2)}, u32[]{:S(2)}) collective-permute-start(s32[1]{0:T(128)} %param.11), channel_id=1, source_target_pairs={{0,1},{1,0},{2,3},{3,2},{4,5},{5,4},{6,7},{7,6},{8,9},{9,8},{10,11... | collective-permute-start | bytes 20 | tf_op jit(solution)/shard_map/ppermute | solution.py:237
  10.7 1.0 %copy-start = (bf16[512,512]{1,0:T(8,128)(2,1)S(1)}, bf16[512,512]{1,0:T(8,128)(2,1)}, u32[]{:S(2)}) copy-start(bf16[512,512]{1,0:T(8,128)(2,1)} %items_far.1) | copy-start | bytes 1572868
  11.7 0.8 %copy-start.2 = (bf16[46,512]{1,0:T(8,128)(2,1)S(1)}, bf16[46,512]{1,0:T(8,128)(2,1)}, u32[]{:S(2)}) copy-start(bf16[46,512]{1,0:T(8,128)(2,1)} %days_far.1) | copy-start | bytes 141316
  12.5 0.7 %copy-start.3 = (s32[3,128]{1,0:T(4,128)S(1)}, s32[3,128]{1,0:T(4,128)}, u32[]{:S(2)}) copy-start(s32[3,128]{1,0:T(4,128)} %index_far.1) | copy-start | bytes 4612
  19.5 21.9 %copy-start.1 = (f32[8,512]{1,0:T(8,128)S(1)}, f32[8,512]{1,0:T(8,128)}, u32[]{:S(2)}) copy-start(f32[8,512]{1,0:T(8,128)} %refs_1_.1) | copy-start | bytes 49156
where the time goes:
time: 42.4 us; the launch traced here: 42 us
  blocking collectives  16.7 us (39%)
  Pallas kernels  8.6 us (20%)
  starting transfers between devices  8.24 us (19%)
  waiting for transfers between devices  3.83 us (9%)
  local copies, waits for them, and re-layouts  3.24 us (8%)
  other arithmetic  0.72 us (2%)
  between operations  0.69 us (2%)
    all_to_all x1, blocking collectives, per_device(): received = lax.all_to_all(partial, axes, 0, 0, tiled=True)  16.7 us
    all_to_all x1, starting transfers between devices, per_device(): lax.all_to_all(spread, axes, 0, 0, tiled=True).reshape(devices * own, rank)  6.96 us
    pallas_call x1, Pallas kernels, per_device(): pl.pallas_call(tiles_kernel, out_shape=jax.ShapeDtypeStruct((devices, own...  5.17 us
    all_to_all x1, waiting for transfers between devices, per_device(): lax.all_to_all(spread, axes, 0, 0, tiled=True).reshape(devices * own, rank)  3.49 us
    pallas_call x1, Pallas kernels, per_device(): pl.pallas_call(plan_kernel, out_shape=(jax.ShapeDtypeStruct(plan_shape, j...  2.75 us
    unnamed x8, local copies, waits for them, and re-layouts  2.52 us
    ppermute x4, starting transfers between devices, per_device(): lax.ppermute(x, 'day', mates)  1.28 us
  transfers between devices with their start and end apart: 5, of which 2 were waited for; matrix products, arithmetic and copies ran while one was open for 3% of the time, Pallas kernels for 7%

commit v1 on v0

--- a/solution.py
+++ b/solution.py
@@ -1,3 +1,5 @@
+import functools
+
 import jax
 import jax.numpy as jnp
 from jax import lax
@@ -11,8 +13,12 @@
 CHUNK = 16
 LANES = 128
 NEEDS = 8
+DAY_ROW = 4
+FIRST = 2
+PLAN_MIB = 50
 VMEM = pl.BlockSpec(memory_space=pltpu.VMEM)
 SMEM = pl.BlockSpec(memory_space=pltpu.SMEM)
+ANY = pl.BlockSpec(memory_space=pl.ANY)
 HBM = pl.BlockSpec(memory_space=pltpu.HBM)
 MIB = 1024 * 1024
 
@@ -22,11 +28,10 @@
 
 
 def plan_kernel(
-    index_far, live_far, days_far, mate_index_far, mate_live_far, mate_days_far, items_far,
-    plan, items, day_rows, extra,
+    index_far, live_far, days_far, mate_index_far, mate_live_far, mate_days_far, items_far, counts_far,
+    plan, items, day_rows, first_counts,
     index, live, days, mate_index, mate_live, mate_days, spots, sems,
 ):
-    rank = items.shape[1]
     fetch = [
         pltpu.make_async_copy(far, near, sems.at[i])
         for i, (far, near) in enumerate(
@@ -38,6 +43,7 @@
                 (days_far, days),
                 (mate_days_far, mate_days),
                 (items_far, items),
+                (counts_far.at[pl.ds(0, first_counts.shape[0])], first_counts),
             )
         )
     ]
@@ -60,7 +66,7 @@
     mine, other = live[0], mate_live[0]
     half = (mine + other + 1) >> 1
     keep, mate_keep = jnp.minimum(mine, half), jnp.minimum(other, half)
-    parts = jnp.maximum((keep + CHUNK - 1) // CHUNK, 2)
+    parts = jnp.maximum((keep + CHUNK - 1) // CHUNK, FIRST)
     mate_first = mate_keep // CHUNK
     mate_parts = jnp.where(mate_keep < other, (other + CHUNK - 1) // CHUNK - mate_first, 0)
     plan[0, 1] = parts
@@ -99,36 +105,43 @@
     used = enlist(
         mate_index, mate_keep, other, (parts - mate_first) * CHUNK, day_rows.shape[0] // 2, used
     )
-    plan[0, 0] = (used + UNROLL - 1) // UNROLL
+    plan[0, 0] = used
 
     for copy in fetch[4:]:
         copy.wait()
+    day_rows[...] = jnp.zeros_like(day_rows)
     count = days.shape[0]
     day_rows[0:count, :] = days[...].astype(jnp.float32)
     day_rows[day_rows.shape[0] // 2 : day_rows.shape[0] // 2 + count, :] = mate_days[...].astype(
         jnp.float32
     )
-    day_sum = jnp.sum(days[...].astype(jnp.float32), axis=0, keepdims=True)
+
+
+def sums_kernel(chips, kept, items, day_rows, extra):
+    rank = items.shape[1]
+    day_sum = jnp.sum(day_rows[...], axis=0, keepdims=True)
     item_sum = jnp.sum(items[...].astype(jnp.float32), axis=0, keepdims=True)
-    item_at, day_at = lax.axis_index("item"), lax.axis_index("day")
+    item_at, chip_at = lax.axis_index("item"), lax.axis_index("day") >> 1
     row = lax.broadcasted_iota(jnp.int32, (8, LANES), 0)
     block = jnp.zeros((8, LANES), jnp.float32)
     for q in range(rank // LANES):
-        for first, total, at in ((0, item_sum, day_at), (2, day_sum, item_at)):
-            part = jnp.where(at == q, total[:, q * LANES : (q + 1) * LANES], 0.0)
+        for first, total, here in (
+            (2 * (q // chips), item_sum, chip_at == q % chips),
+            (DAY_ROW, day_sum, item_at == q),
+        ):
+            part = jnp.where(here, total[:, q * LANES : (q + 1) * LANES], 0.0)
             high = part.astype(jnp.bfloat16).astype(jnp.float32)
             block = jnp.where(row == first, block + high, block)
             block = jnp.where(row == first + 1, block + (part - high), block)
-    extra[...] = block
+    extra[...] = block.astype(jnp.bfloat16)
 
 
 def tiles_kernel(
-    plan_far, counts_far, mate_counts_far, users, items, day_rows, extra,
-    out,
+    plan_far, counts_far, mate_counts_far, first_counts, users, items, day_rows,
+    kept, sent,
     plan, counts, phi, plan_sem, counts_sem, *buffers,
 ):
     weighted, ratios = buffers[:UNROLL], buffers[UNROLL:]
-    rank = users.shape[1]
     fetch = pltpu.make_async_copy(plan_far, plan, plan_sem)
     fetch.start()
 
@@ -137,13 +150,12 @@
         target = counts.at[pl.ds(pl.multiple_of(at * CHUNK, CHUNK), CHUNK)]
         return pltpu.make_async_copy(source, target, counts_sem.at[at])
 
-    part(counts_far, 0, 0).start()
-    part(counts_far, 1, 1).start()
+    counts[0 : FIRST * CHUNK] = first_counts[...]
     phi[...] = jnp.zeros_like(phi)
     weighted[-1][...] = jnp.zeros_like(weighted[-1])
     ratios[-1][...] = jnp.zeros_like(ratios[-1])
     fetch.wait()
-    turns, parts, mate_first, all_parts = plan[0, 0], plan[0, 1], plan[0, 2], plan[0, 3]
+    groups, parts, mate_first, all_parts = plan[0, 0], plan[0, 1], plan[0, 2], plan[0, 3]
 
     def start_part(c, carry):
         part(counts_far, c, c).start()
@@ -157,11 +169,8 @@
         part(counts_far, 0, c).wait()
         return carry
 
-    lax.fori_loop(2, parts, start_part, 0)
+    lax.fori_loop(FIRST, parts, start_part, 0)
     lax.fori_loop(parts, all_parts, start_mate_part, 0)
-    out[:, :, rank:] = jnp.broadcast_to(
-        extra[...].astype(jnp.bfloat16)[None], (out.shape[0], 8, LANES)
-    )
 
     def code_at(spot):
         return plan[1 + (spot >> 7), spot & (LANES - 1)]
@@ -199,24 +208,49 @@
             add_terms(jnp.maximum(g - 1, 0), (i - 1) % UNROLL)
         return need
 
-    ready = lax.fori_loop(0, turns, turn, jnp.int32(0))
+    rest = groups & (UNROLL - 1)
+    turns = (groups >> 2) + (rest == UNROLL - 1).astype(jnp.int32)
+    ready = lax.fori_loop(0, turns, turn, jnp.int32(FIRST))
     lax.fori_loop(ready, all_parts, wait_part, 0)
-    add_terms(jnp.maximum(turns * UNROLL - 1, 0), UNROLL - 1)
-    out[:, :, 0:rank] = phi[...].reshape(out.shape[0], out.shape[1], rank).astype(jnp.bfloat16)
-
-
-def finish_kernel(n_item, n_day, received, user_factors, out):
+    g = turns * UNROLL
+
+    @pl.when((rest == 1) | (rest == 2))
+    def _():
+        make_ratio(g, 0)
+        add_terms(jnp.maximum(g - 1, 0), UNROLL - 1)
+        add_terms(g, 0)
+
+    @pl.when((rest != 1) & (rest != 2))
+    def _():
+        add_terms(jnp.maximum(g - 1, 0), UNROLL - 1)
+
+    @pl.when(rest == 2)
+    def _():
+        make_ratio(g + 1, 1)
+        add_terms(g + 1, 1)
+
+    own = kept.shape[1]
+    core = lax.axis_index("day") & 1
+    for j in range(kept.shape[0]):
+        kept[j] = phi[pl.ds(pl.multiple_of((2 * j + core) * own, own), own), :]
+        sent[j] = phi[pl.ds(pl.multiple_of((2 * j + 1 - core) * own, own), own), :]
+
+
+def finish_kernel(n_item, chips, received, user_factors, out):
     rank = user_factors.shape[1]
     phi = jnp.sum(received[:, :, 0:rank].astype(jnp.float32), axis=0)
     for q in range(rank // LANES):
         cols = slice(q * LANES, (q + 1) * LANES)
-        item = received[q, :, rank:].astype(jnp.float32)
+        item = received[q % chips, :, rank:].astype(jnp.float32)
         for i in range(1, n_item):
-            item = item + received[i * n_day + q, :, rank:].astype(jnp.float32)
-        day = received[q * n_day, :, rank:].astype(jnp.float32)
-        for k in range(1, n_day):
-            day = day + received[q * n_day + k, :, rank:].astype(jnp.float32)
-        totals = (item[0:1] + item[1:2]) * (day[2:3] + day[3:4])
+            item = item + received[i * chips + q % chips, :, rank:].astype(jnp.float32)
+        day = received[q * chips, :, rank:].astype(jnp.float32)
+        for k in range(1, chips):
+            day = day + received[q * chips + k, :, rank:].astype(jnp.float32)
+        at = 2 * (q // chips)
+        totals = (item[at : at + 1] + item[at + 1 : at + 2]) * (
+            day[DAY_ROW : DAY_ROW + 1] + day[DAY_ROW + 1 : DAY_ROW + 2]
+        )
         out[:, cols] = user_factors[:, cols] * phi[:, cols] / totals
 
 
@@ -239,15 +273,15 @@
         )
         spread = jnp.broadcast_to(user_factors.astype(jnp.bfloat16)[None], (devices, own, rank))
         gathered = lax.all_to_all(spread, axes, 0, 0, tiled=True).reshape(devices * own, rank)
-        plan, items, day_rows, extra = pl.pallas_call(
+        plan, items, day_rows, first_counts = pl.pallas_call(
             plan_kernel,
             out_shape=(
                 jax.ShapeDtypeStruct(plan_shape, jnp.int32),
                 jax.ShapeDtypeStruct(item_factors.shape, jnp.bfloat16),
                 jax.ShapeDtypeStruct((2 * day_space, rank), jnp.float32),
-                jax.ShapeDtypeStruct((8, LANES), jnp.float32),
+                jax.ShapeDtypeStruct((FIRST * CHUNK, *tile_counts.shape[1:]), jnp.bfloat16),
             ),
-            in_specs=[HBM] * 7,
+            in_specs=[HBM] * 8,
             out_specs=(SMEM, VMEM, VMEM, VMEM),
             scratch_shapes=[
                 pltpu.SMEM(tile_index.shape, jnp.int32),
@@ -257,15 +291,17 @@
                 pltpu.SMEM(tile_live.shape, jnp.int32),
                 pltpu.VMEM(day_factors.shape, jnp.bfloat16),
                 pltpu.SMEM((blocks,), jnp.int32),
-                pltpu.SemaphoreType.DMA((7,)),
+                pltpu.SemaphoreType.DMA((8,)),
             ],
-            compiler_params=pltpu.CompilerParams(vmem_limit_bytes=16 * MIB),
-        )(tile_index, tile_live, day_factors, mate_index, mate_live, mate_days, item_factors)
-        partial = pl.pallas_call(
+            compiler_params=pltpu.CompilerParams(vmem_limit_bytes=PLAN_MIB * MIB),
+        )(
+            tile_index, tile_live, day_factors, mate_index, mate_live, mate_days, item_factors, tile_counts
+        )
+        kept, sent = pl.pallas_call(
             tiles_kernel,
-            out_shape=jax.ShapeDtypeStruct((devices, own, rank + LANES), jnp.bfloat16),
+            out_shape=(jax.ShapeDtypeStruct((devices // 2, own, rank), jnp.float32),) * 2,
             in_specs=[HBM, HBM, HBM, VMEM, VMEM, VMEM, VMEM],
-            out_specs=VMEM,
+            out_specs=(VMEM, VMEM),
             scratch_shapes=[
                 pltpu.SMEM(plan_shape, jnp.int32),
                 pltpu.VMEM((cap + 2 * CHUNK, *tile_counts.shape[1:]), jnp.bfloat16),
@@ -276,10 +312,26 @@
             + [pltpu.VMEM((GROUP * TILE, rank), jnp.bfloat16)] * UNROLL
             + [pltpu.VMEM((TILE, GROUP * TILE), jnp.bfloat16)] * UNROLL,
             compiler_params=pltpu.CompilerParams(vmem_limit_bytes=51 * MIB),
-        )(plan, tile_counts, mate_counts, gathered, items, day_rows, extra)
-        received = lax.all_to_all(partial, axes, 0, 0, tiled=True)
+        )(plan, tile_counts, mate_counts, first_counts, gathered, items, day_rows)
+        chip_sum = (kept + lax.ppermute(sent, "day", mates)).astype(jnp.bfloat16)
+        extra = pl.pallas_call(
+            functools.partial(sums_kernel, n_day // 2),
+            out_shape=jax.ShapeDtypeStruct((8, LANES), jnp.bfloat16),
+            in_specs=[ANY, VMEM, VMEM],
+            out_specs=VMEM,
+            compiler_params=pltpu.CompilerParams(vmem_limit_bytes=16 * MIB),
+        )(kept, items, day_rows)
+        sums = jnp.broadcast_to(extra[None], (devices // 2, 8, LANES))
+        received = lax.all_to_all(
+            jnp.concatenate([chip_sum, sums], axis=2),
+            axes,
+            0,
+            0,
+            axis_index_groups=[list(range(c, devices, 2)) for c in range(2)],
+            tiled=True,
+        )
         return pl.pallas_call(
-            lambda *refs: finish_kernel(n_item, n_day, *refs),
+            functools.partial(finish_kernel, n_item, n_day // 2),
             out_shape=jax.ShapeDtypeStruct((own, rank), jnp.float32),
             in_specs=[VMEM, VMEM],
             out_specs=VMEM,

time: 42.4 us -> 40.8 us (0.962)
  blocking collectives: 16.7 us -> 13.8 us
  waiting for transfers between devices: 3.83 us -> 5.28 us
  Pallas kernels: 8.6 us -> 8.08 us
    all_to_all x1, blocking collectives: 16.7 us -> 13.8 us  [per_device(): lax.all_to_all(jnp.concatenate([chip_sum, sums], axis=2), axes, 0, 0, axi...]
    ppermute x0 -> x1, waiting for transfers between devices: none -> 1.41 us  [per_device(): chip_sum = (kept + lax.ppermute(sent, 'day', mates)).astype(jnp.bfloat16)]
    pallas_call x2 -> x3, Pallas kernels: 5.85 us -> 5.36 us  [the longest x1 4.61 us: per_device(): pl.pallas_call(tiles_kernel, out_shape=(jax.ShapeDtypeStruct((devices //...]
  transfers between devices with their start and end apart: 5 -> 6, of which waited for: 2 -> 3; matrix products, arithmetic and copies ran while one was open for 3% -> 4% of each run, Pallas kernels for 7% -> 7%
where the time goes in v1:
time: 40.8 us; the launch traced here: 40.2 us
  blocking collectives  13.8 us (34%)
  starting transfers between devices  8.31 us (20%)
  Pallas kernels  8.08 us (20%)
  waiting for transfers between devices  5.28 us (13%)
  local copies, waits for them, and re-layouts  3.25 us (8%)
  other arithmetic  0.77 us (2%)
  between operations  0.72 us (2%)
    all_to_all x1, blocking collectives, per_device(): lax.all_to_all(jnp.concatenate([chip_sum, sums], axis=2), axes, 0, 0, axi...  13.8 us
    all_to_all x1, starting transfers between devices, per_device(): lax.all_to_all(spread, axes, 0, 0, tiled=True).reshape(devices * own, rank)  6.96 us
    pallas_call x1, Pallas kernels, per_device(): pl.pallas_call(tiles_kernel, out_shape=(jax.ShapeDtypeStruct((devices //...  4.61 us
    all_to_all x1, waiting for transfers between devices, per_device(): lax.all_to_all(spread, axes, 0, 0, tiled=True).reshape(devices * own, rank)  3.38 us
    pallas_call x1, Pallas kernels, per_device(): pl.pallas_call(plan_kernel, out_shape=(jax.ShapeDtypeStruct(plan_shape, j...  2.72 us
    unnamed x8, local copies, waits for them, and re-layouts  2.52 us
    ppermute x1, waiting for transfers between devices, per_device(): chip_sum = (kept + lax.ppermute(sent, 'day', mates)).astype(jnp.bfloat16)  1.41 us
    ppermute x4, starting transfers between devices, per_device(): lax.ppermute(x, 'day', mates)  1.28 us
  transfers between devices with their start and end apart: 6, of which 3 were waited for; matrix products, arithmetic and copies ran while one was open for 4% of the time, Pallas kernels for 7%

profile of v1, /device:TPU:0, one launch (start us, length us, event | category | flops | bytes accessed | tf_op | source)
XLA Modules:
  0.0 40.2 jit_solution(11651115509642306462)
XLA Ops:
  0.0 0.5 %collective-permute-start.3 = (bf16[128,128,128]{2,1,0:T(8,128)(2,1)}, bf16[128,128,128]{2,1,0:T(8,128)(2,1)}, u32[]{:S(2)}, u32[]{:S(2)}) collective-permute-start(bf16[128,128,128]{2,1,0:T(8,128)(2,1)} %counts_far.3), channel_id=1, source_target_pairs={{0,1},{1,0},{2,3},{3,2},{4,5},{5,4},{6,7},{7,6},{8,9},{9,8},{10,11... | collective-permute-start | bytes 12582920 | tf_op jit(solution)/shard_map/ppermute | solution.py:271
  0.5 0.7 %convert_element_type.6 = bf16[8,512]{1,0:T(8,128)(2,1)S(1)} convert(f32[8,512]{1,0:T(8,128)} %user_factors.1) | non-fusion elementwise | flops 4096 | bytes 24576 | tf_op jit(solution)/shard_map/convert_element_type | solution.py:274
  1.2 0.7 %broadcast_in_dim.4 = bf16[32,8,512]{2,1,0:T(8,128)(2,1)} broadcast(bf16[8,512]{1,0:T(8,128)(2,1)S(1)} %convert_element_type.6), dimensions={1,2} | broadcast | bytes 270336 | tf_op jit(solution)/shard_map/broadcast_in_dim | solution.py:274
  1.9 7.0 %all-to-all-start = ((bf16[32,8,512]{2,1,0:T(8,128)(2,1)}), bf16[32,8,512]{2,1,0:T(8,128)(2,1)S(1)}, u32[]{:S(2)}, u32[]{:S(2)}) async-start(bf16[32,8,512]{2,1,0:T(8,128)(2,1)} %broadcast_in_dim.4), calls=%async_computation | async-start | bytes 524288 | tf_op jit(solution)/shard_map/all_to_all | solution.py:275
  8.9 0.3 collective-permute-start.2
  9.2 0.3 collective-permute-start
  9.4 0.3 collective-permute-start.1
  10.3 0.5 %collective-permute-done.1.mate_live_far = s32[1]{0:T(128)} collective-permute-done((s32[1]{0:T(128)}, s32[1]{0:T(128)}, u32[]{:S(2)}, u32[]{:S(2)}) %collective-permute-start.1) | collective-permute-done | bytes 36 | tf_op jit(solution)/shard_map/ppermute | solution.py:271
  10.8 0.0 collective-permute-done.mate_index_far
  10.8 0.0 collective-permute-done.2.mate_days_far
  10.8 0.0 copy-start
  10.8 1.0 %copy-done = bf16[512,512]{1,0:T(8,128)(2,1)S(1)} copy-done((bf16[512,512]{1,0:T(8,128)(2,1)S(1)}, bf16[512,512]{1,0:T(8,128)(2,1)}, u32[]{:S(2)}) %copy-start) | copy-done | bytes 524312
  11.9 0.0 copy-start.2
  11.9 0.8 %copy-done.2 = bf16[46,512]{1,0:T(8,128)(2,1)S(1)} copy-done((bf16[46,512]{1,0:T(8,128)(2,1)S(1)}, bf16[46,512]{1,0:T(8,128)(2,1)}, u32[]{:S(2)}) %copy-start.2) | copy-done | bytes 47128
  12.7 0.0 copy-start.3
  12.7 0.7 %copy-done.3 = s32[3,128]{1,0:T(4,128)S(1)} copy-done((s32[3,128]{1,0:T(4,128)S(1)}, s32[3,128]{1,0:T(4,128)}, u32[]{:S(2)}) %copy-start.3) | copy-done | bytes 1560
  13.4 2.7 %shard_map.64 = (s32[3,128]{1,0:T(4,128)S(1)}, bf16[512,512]{1,0:T(8,128)(2,1)S(1)}, f32[96,512]{1,0:T(8,128)S(1)}, bf16[32,128,128]{2,1,0:T(8,128)(2,1)S(1)}) custom-call(s32[3,128]{1,0:T(4,128)S(1)} %copy-done.3, s32[1]{0:T(128)S(6)} %copy.7.live_far, bf16[46,512]{1,0:T(8,128)(2,1)S(1)} %copy-done.2, s32[3,128]{1,0:T(4,128)S(1)} %collective-permute-done.mate_index_far, ...), custom_call_target="tpu_custom_call" | custom-call | tf_op jit(solution)/shard_map/pallas_call | solution.py:276
  16.1 3.4 %all-to-all-done = bf16[32,8,512]{2,1,0:T(8,128)(2,1)S(1)} async-done(((bf16[32,8,512]{2,1,0:T(8,128)(2,1)}), bf16[32,8,512]{2,1,0:T(8,128)(2,1)S(1)}, u32[]{:S(2)}, u32[]{:S(2)}) %all-to-all-start) | async-done | bytes 262176 | tf_op jit(solution)/shard_map/all_to_all | solution.py:275
  19.5 0.0 collective-permute-done.3.mate_counts_far
  19.5 0.0 copy-start.1
  19.5 4.6 %shard_map.65 = (f32[16,8,512]{2,1,0:T(8,128)S(1)}, f32[16,8,512]{2,1,0:T(8,128)S(1)}) custom-call(s32[3,128]{1,0:T(4,128)S(1)} %get-tuple-element.11.plan_far, bf16[128,128,128]{2,1,0:T(8,128)(2,1)} %counts_far.3, bf16[128,128,128]{2,1,0:T(8,128)(2,1)} %collective-permute-done.3.mate_counts_far, bf16[32,128,128]{2,1,0:T(8,128)(2,1)S(1)} %get-tuple-element.12.first_counts, ...), custom_call_target="tpu_custom_call" | custom-call | tf_op jit(solution)/shard_map/pallas_call | solution.py:300
  24.1 0.1 collective-permute-start.4
  24.2 0.1 shard_map.66
  24.3 1.4 %collective-permute-done.4 = f32[16,8,512]{2,1,0:T(8,128)S(1)} collective-permute-done((f32[16,8,512]{2,1,0:T(8,128)S(1)}, f32[16,8,512]{2,1,0:T(8,128)S(1)}, u32[]{:S(2)}, u32[]{:S(2)}) %collective-permute-start.4) | collective-permute-done | bytes 262176 | tf_op jit(solution)/shard_map/ppermute | solution.py:316
  25.8 13.8 %all_to_all.10.received = bf16[16,8,640]{2,1,0:T(8,128)(2,1)S(1)} all-to-all(bf16[16,8,640]{2,1,0:T(8,128)(2,1)S(1)} %pad_maximum_fusion), channel_id=1, replica_groups={{0,2,4,6,8,10,12,14,16,18,20,22,24,26,28,30},{1,3,5,7,9,11,13,15,17,19,..., dimensions={0} | all-to-all | bytes 327680 | tf_op jit(solution)/shard_map/all_to_all | solution.py:325
  39.6 0.0 copy-done.1
  39.6 0.6 %shard_map.67 = f32[8,512]{1,0:T(8,128)} custom-call(bf16[16,8,640]{2,1,0:T(8,128)(2,1)S(1)} %all_to_all.10.received, f32[8,512]{1,0:T(8,128)S(1)} %copy-done.1), custom_call_target="tpu_custom_call" | custom-call | tf_op jit(solution)/shard_map/pallas_call | solution.py:333
  (3 shorter events, 0.1 us)
Async XLA Ops:
  0.0 19.5 %collective-permute-start.3 = (bf16[128,128,128]{2,1,0:T(8,128)(2,1)}, bf16[128,128,128]{2,1,0:T(8,128)(2,1)}, u32[]{:S(2)}, u32[]{:S(2)}) collective-permute-start(bf16[128,128,128]{2,1,0:T(8,128)(2,1)} %counts_far.3), channel_id=1, source_target_pairs={{0,1},{1,0},{2,3},{3,2},{4,5},{5,4},{6,7},{7,6},{8,9},{9,8},{10,11... | collective-permute-start | bytes 12582920 | tf_op jit(solution)/shard_map/ppermute | solution.py:271
  1.9 17.6 %all-to-all-start = ((bf16[32,8,512]{2,1,0:T(8,128)(2,1)}), bf16[32,8,512]{2,1,0:T(8,128)(2,1)S(1)}, u32[]{:S(2)}, u32[]{:S(2)}) async-start(bf16[32,8,512]{2,1,0:T(8,128)(2,1)} %broadcast_in_dim.4), calls=%async_computation | async-start | bytes 524288 | tf_op jit(solution)/shard_map/all_to_all | solution.py:275
  8.9 2.0 %collective-permute-start.2 = (bf16[46,512]{1,0:T(8,128)(2,1)}, bf16[46,512]{1,0:T(8,128)(2,1)S(1)}, u32[]{:S(2)}, u32[]{:S(2)}) collective-permute-start(bf16[46,512]{1,0:T(8,128)(2,1)} %days_far.1), channel_id=1, source_target_pairs={{0,1},{1,0},{2,3},{3,2},{4,5},{5,4},{6,7},{7,6},{8,9},{9,8},{10,11... | collective-permute-start | bytes 141320 | tf_op jit(solution)/shard_map/ppermute | solution.py:271
  9.2 1.6 %collective-permute-start = (s32[3,128]{1,0:T(4,128)}, s32[3,128]{1,0:T(4,128)S(1)}, u32[]{:S(2)}, u32[]{:S(2)}) collective-permute-start(s32[3,128]{1,0:T(4,128)} %index_far.1), channel_id=1, source_target_pairs={{0,1},{1,0},{2,3},{3,2},{4,5},{5,4},{6,7},{7,6},{8,9},{9,8},{10,11... | collective-permute-start | bytes 4616 | tf_op jit(solution)/shard_map/ppermute | solution.py:271
  9.4 1.4 %collective-permute-start.1 = (s32[1]{0:T(128)}, s32[1]{0:T(128)}, u32[]{:S(2)}, u32[]{:S(2)}) collective-permute-start(s32[1]{0:T(128)} %param.11), channel_id=1, source_target_pairs={{0,1},{1,0},{2,3},{3,2},{4,5},{5,4},{6,7},{7,6},{8,9},{9,8},{10,11... | collective-permute-start | bytes 20 | tf_op jit(solution)/shard_map/ppermute | solution.py:271
  10.8 1.0 %copy-start = (bf16[512,512]{1,0:T(8,128)(2,1)S(1)}, bf16[512,512]{1,0:T(8,128)(2,1)}, u32[]{:S(2)}) copy-start(bf16[512,512]{1,0:T(8,128)(2,1)} %items_far.1) | copy-start | bytes 1572868
  11.9 0.8 %copy-start.2 = (bf16[46,512]{1,0:T(8,128)(2,1)S(1)}, bf16[46,512]{1,0:T(8,128)(2,1)}, u32[]{:S(2)}) copy-start(bf16[46,512]{1,0:T(8,128)(2,1)} %days_far.1) | copy-start | bytes 141316
  12.7 0.7 %copy-start.3 = (s32[3,128]{1,0:T(4,128)S(1)}, s32[3,128]{1,0:T(4,128)}, u32[]{:S(2)}) copy-start(s32[3,128]{1,0:T(4,128)} %index_far.1) | copy-start | bytes 4612
  19.5 20.1 %copy-start.1 = (f32[8,512]{1,0:T(8,128)S(1)}, f32[8,512]{1,0:T(8,128)}, u32[]{:S(2)}) copy-start(f32[8,512]{1,0:T(8,128)} %user_factors.1) | copy-start | bytes 49156
  24.1 1.6 %collective-permute-start.4 = (f32[16,8,512]{2,1,0:T(8,128)S(1)}, f32[16,8,512]{2,1,0:T(8,128)S(1)}, u32[]{:S(2)}, u32[]{:S(2)}) collective-permute-start(f32[16,8,512]{2,1,0:T(8,128)S(1)} %get-tuple-element.16), channel_id=1, source_target_pairs={{0,1},{1,0},{2,3},{3,2},{4,5},{5,4},{6,7},{7,6},{8,9},{9,8},{10,11... | collective-permute-start | bytes 786440 | tf_op jit(solution)/shard_map/ppermute | solution.py:316

commit v2 on v1

--- a/solution.py
+++ b/solution.py
@@ -14,7 +14,7 @@
 LANES = 128
 NEEDS = 8
 DAY_ROW = 4
-FIRST = 2
+FIRST = 3
 PLAN_MIB = 50
 VMEM = pl.BlockSpec(memory_space=pltpu.VMEM)
 SMEM = pl.BlockSpec(memory_space=pltpu.SMEM)
@@ -28,20 +28,15 @@
 
 
 def plan_kernel(
-    index_far, live_far, days_far, mate_index_far, mate_live_far, mate_days_far, items_far, counts_far,
-    plan, items, day_rows, first_counts,
-    index, live, days, mate_index, mate_live, mate_days, spots, sems,
+    blocks, live, mate_live, index, mate_index, mate_days, days_far, items_far, counts_far,
+    plan, items, across, day_rows, first_counts,
+    days, sems,
 ):
     fetch = [
         pltpu.make_async_copy(far, near, sems.at[i])
         for i, (far, near) in enumerate(
             (
-                (index_far, index),
-                (live_far, live),
-                (mate_index_far, mate_index),
-                (mate_live_far, mate_live),
                 (days_far, days),
-                (mate_days_far, mate_days),
                 (items_far, items),
                 (counts_far.at[pl.ds(0, first_counts.shape[0])], first_counts),
             )
@@ -49,19 +44,6 @@
     ]
     for copy in fetch:
         copy.start()
-
-    def clear(i, carry):
-        for j in range(LANES):
-            plan[i, j] = -1
-        return carry
-
-    lax.fori_loop(1, plan.shape[0], clear, 0)
-    for j in range(LANES):
-        plan[0, j] = 0
-    for u in range(spots.shape[0]):
-        spots[u] = 0
-    for copy in fetch[:4]:
-        copy.wait()
 
     mine, other = live[0], mate_live[0]
     half = (mine + other + 1) >> 1
@@ -69,52 +51,81 @@
     parts = jnp.maximum((keep + CHUNK - 1) // CHUNK, FIRST)
     mate_first = mate_keep // CHUNK
     mate_parts = jnp.where(mate_keep < other, (other + CHUNK - 1) // CHUNK - mate_first, 0)
-    plan[0, 1] = parts
-    plan[0, 2] = mate_first
-    plan[0, 3] = parts + mate_parts
-
-    def enlist(table, low, high, shift, day_shift, used):
-        def place(u, code, tile, used):
-            spot = spots[u]
-            new = (spot & (GROUP - 1)) == 0
-            spot = jnp.where(new, used * GROUP, spot)
-            spots[u] = spot + 1
-            plan[1 + (spot >> 7), spot & (LANES - 1)] = code
-            plan[0, NEEDS + spot // (GROUP * UNROLL)] = (tile >> 4) + 1
-            return used + new.astype(jnp.int32)
-
-        def read(s):
-            u, tile = table[0, s], s + shift
-            code = (u << 24) | (tile << 16) | (table[1, s] << 8) | (table[2, s] + day_shift)
-            return u, code, tile
-
-        def four(t, used):
-            found = [read(low + t * 4 + j) for j in range(4)]
-            for u, code, tile in found:
-                used = place(u, code, tile, used)
-            return used
-
-        def one(s, used):
-            return place(*read(s), used)
-
-        fours = (high - low) >> 2
-        used = lax.fori_loop(0, fours, four, used)
-        return lax.fori_loop(low + fours * 4, high, one, used)
-
-    used = enlist(index, 0, keep, 0, 0, jnp.int32(0))
-    used = enlist(
-        mate_index, mate_keep, other, (parts - mate_first) * CHUNK, day_rows.shape[0] // 2, used
+
+    def iota(rows, columns, axis):
+        return lax.broadcasted_iota(jnp.int32, (rows, columns), axis)
+
+    def both(row):
+        return jnp.concatenate([index[row : row + 1, :], mate_index[row : row + 1, :]], axis=1)
+
+    cap = index.shape[1]
+    wide = 2 * cap
+    lane = iota(1, wide, 1)
+    from_mate = lane >= cap
+    slot = jnp.where(from_mate, lane - cap, lane)
+    low, high = jnp.where(from_mate, mate_keep, 0), jnp.where(from_mate, other, keep)
+    active = (slot >= low) & (slot < high)
+    tile = slot + jnp.where(from_mate, (parts - mate_first) * CHUNK, 0)
+    day = both(2) + jnp.where(from_mate, day_rows.shape[0] // 2, 0)
+    user = jnp.where(active, both(0), -1)
+
+    height = round_up(blocks, 16)
+    hot = jnp.where(iota(height, wide, 0) == user, 1.0, 0.0)
+    earlier = jnp.where(iota(wide, wide, 0) < iota(wide, wide, 1), 1.0, 0.0)
+    rank = jnp.dot(
+        hot.astype(jnp.bfloat16), earlier.astype(jnp.bfloat16), preferred_element_type=jnp.float32
     )
-    plan[0, 0] = used
-
-    for copy in fetch[4:]:
-        copy.wait()
+    sizes = jnp.sum(hot, axis=1, keepdims=True).astype(jnp.int32)
+    groups = ((sizes + GROUP - 1) // GROUP).astype(jnp.float32)
+    below = jnp.where(iota(height, height, 1) < iota(height, height, 0), 1.0, 0.0)
+    before = jnp.dot(
+        below.astype(jnp.bfloat16),
+        jnp.broadcast_to(groups, (height, LANES)).astype(jnp.bfloat16),
+        preferred_element_type=jnp.float32,
+    )[:, 0:1]
+    spot = jnp.sum(hot * (GROUP * before + rank), axis=0, keepdims=True).astype(jnp.int32)
+    spot = jnp.where(active, spot, -1)
+
+    rows = plan.shape[0] - 1
+    taken = jnp.where(iota(rows * LANES, wide, 0) == spot, 1.0, 0.0).astype(jnp.bfloat16)
+    field = iota(16, wide, 0)
+    fields = jnp.zeros((16, wide), jnp.int32)
+    for k, value in enumerate((user, tile, both(1), day, jnp.ones_like(user))):
+        fields = jnp.where(field == k, value, fields)
+    found = lax.dot_general(
+        fields.astype(jnp.float32).astype(jnp.bfloat16),
+        taken,
+        (((1,), (1,)), ((), ())),
+        preferred_element_type=jnp.float32,
+    ).astype(jnp.int32)
+    code = (found[0:1] << 24) | (found[1:2] << 16) | (found[2:3] << 8) | found[3:4]
+    code = jnp.where(found[4:5] > 0, code, -1)
+    for k in range(rows):
+        plan[1 + k : 2 + k, :] = code[:, k * LANES : (k + 1) * LANES]
+
+    turns = round_up(rows * LANES // (GROUP * UNROLL), 8)
+    turn = jnp.floor((spot.astype(jnp.float32) + 0.5) / (GROUP * UNROLL)).astype(jnp.int32)
+    in_turn = iota(turns, wide, 0) == jnp.where(active, turn, -1)
+    need = jnp.max(jnp.where(in_turn, tile // CHUNK + 1, 0), axis=1, keepdims=True)
+    at = iota(1, LANES, 1)
+    head = jnp.sum(
+        jnp.where(iota(turns, LANES, 1) == iota(turns, LANES, 0) + NEEDS, need, 0),
+        axis=0,
+        keepdims=True,
+    )
+    head = jnp.where(at == 0, jnp.sum(groups, axis=0, keepdims=True).astype(jnp.int32), head)
+    for k, value in ((1, parts), (2, mate_first), (3, parts + mate_parts)):
+        head = jnp.where(at == k, value, head)
+    plan[0:1, :] = head
+
+    fetch[0].wait()
     day_rows[...] = jnp.zeros_like(day_rows)
-    count = days.shape[0]
+    count, space = days.shape[0], day_rows.shape[0] // 2
     day_rows[0:count, :] = days[...].astype(jnp.float32)
-    day_rows[day_rows.shape[0] // 2 : day_rows.shape[0] // 2 + count, :] = mate_days[...].astype(
-        jnp.float32
-    )
+    day_rows[space : space + count, :] = mate_days[...].astype(jnp.float32)
+    fetch[1].wait()
+    across[...] = items[...].astype(jnp.float32).T.astype(jnp.bfloat16)
+    fetch[2].wait()
 
 
 def sums_kernel(chips, kept, items, day_rows, extra):
@@ -137,7 +148,7 @@
 
 
 def tiles_kernel(
-    plan_far, counts_far, mate_counts_far, first_counts, users, items, day_rows,
+    plan_far, counts_far, mate_counts_far, first_counts, users, items, across, day_rows,
     kept, sent,
     plan, counts, phi, plan_sem, counts_sem, *buffers,
 ):
@@ -186,13 +197,13 @@
             item = pl.multiple_of(((slot >> 8) & 255) * TILE, TILE)
             scale = day_rows[pl.ds(slot & 255, 1), :].astype(jnp.bfloat16)
             weighted[i][j * TILE : (j + 1) * TILE, :] = items[pl.ds(item, TILE), :] * scale
-        model = lax.dot_general(
-            rows, weighted[i][...], (((1,), (1,)), ((), ())), preferred_element_type=jnp.float32
-        )
-        for j, slot in enumerate(slots):
-            cols = slice(j * TILE, (j + 1) * TILE)
-            ratio = counts[(slot >> 16) & 255].astype(jnp.float32) / model[:, cols]
-            ratios[i][:, cols] = jnp.where(codes[j] >= 0, ratio, 0.0).astype(jnp.bfloat16)
+            model = jnp.dot(
+                rows * scale, across[:, pl.ds(item, TILE)], preferred_element_type=jnp.float32
+            )
+            ratio = counts[(slot >> 16) & 255].astype(jnp.float32) / model
+            ratios[i][:, j * TILE : (j + 1) * TILE] = jnp.where(codes[j] >= 0, ratio, 0.0).astype(
+                jnp.bfloat16
+            )
 
     def add_terms(g, i):
         phi[block_of(g), :] += jnp.dot(
@@ -208,26 +219,15 @@
             add_terms(jnp.maximum(g - 1, 0), (i - 1) % UNROLL)
         return need
 
-    rest = groups & (UNROLL - 1)
-    turns = (groups >> 2) + (rest == UNROLL - 1).astype(jnp.int32)
+    turns = (groups + UNROLL - 2) // UNROLL
     ready = lax.fori_loop(0, turns, turn, jnp.int32(FIRST))
     lax.fori_loop(ready, all_parts, wait_part, 0)
-    g = turns * UNROLL
-
-    @pl.when((rest == 1) | (rest == 2))
+    add_terms(jnp.maximum(turns * UNROLL - 1, 0), UNROLL - 1)
+
+    @pl.when(groups > turns * UNROLL)
     def _():
-        make_ratio(g, 0)
-        add_terms(jnp.maximum(g - 1, 0), UNROLL - 1)
-        add_terms(g, 0)
-
-    @pl.when((rest != 1) & (rest != 2))
-    def _():
-        add_terms(jnp.maximum(g - 1, 0), UNROLL - 1)
-
-    @pl.when(rest == 2)
-    def _():
-        make_ratio(g + 1, 1)
-        add_terms(g + 1, 1)
+        make_ratio(turns * UNROLL, 0)
+        add_terms(turns * UNROLL, 0)
 
     own = kept.shape[1]
     core = lax.axis_index("day") & 1
@@ -273,34 +273,30 @@
         )
         spread = jnp.broadcast_to(user_factors.astype(jnp.bfloat16)[None], (devices, own, rank))
         gathered = lax.all_to_all(spread, axes, 0, 0, tiled=True).reshape(devices * own, rank)
-        plan, items, day_rows, first_counts = pl.pallas_call(
-            plan_kernel,
+        plan, items, across, day_rows, first_counts = pl.pallas_call(
+            functools.partial(plan_kernel, blocks),
             out_shape=(
                 jax.ShapeDtypeStruct(plan_shape, jnp.int32),
                 jax.ShapeDtypeStruct(item_factors.shape, jnp.bfloat16),
+                jax.ShapeDtypeStruct(item_factors.shape[::-1], jnp.bfloat16),
                 jax.ShapeDtypeStruct((2 * day_space, rank), jnp.float32),
                 jax.ShapeDtypeStruct((FIRST * CHUNK, *tile_counts.shape[1:]), jnp.bfloat16),
             ),
-            in_specs=[HBM] * 8,
-            out_specs=(SMEM, VMEM, VMEM, VMEM),
+            in_specs=[SMEM, SMEM, VMEM, VMEM, VMEM, HBM, HBM, HBM],
+            out_specs=(VMEM, VMEM, VMEM, VMEM, VMEM),
             scratch_shapes=[
-                pltpu.SMEM(tile_index.shape, jnp.int32),
-                pltpu.SMEM(tile_live.shape, jnp.int32),
                 pltpu.VMEM(day_factors.shape, jnp.bfloat16),
-                pltpu.SMEM(tile_index.shape, jnp.int32),
-                pltpu.SMEM(tile_live.shape, jnp.int32),
-                pltpu.VMEM(day_factors.shape, jnp.bfloat16),
-                pltpu.SMEM((blocks,), jnp.int32),
-                pltpu.SemaphoreType.DMA((8,)),
+                pltpu.SemaphoreType.DMA((3,)),
             ],
             compiler_params=pltpu.CompilerParams(vmem_limit_bytes=PLAN_MIB * MIB),
         )(
-            tile_index, tile_live, day_factors, mate_index, mate_live, mate_days, item_factors, tile_counts
+            tile_live, mate_live, tile_index, mate_index, mate_days,
+            day_factors, item_factors, tile_counts,
         )
         kept, sent = pl.pallas_call(
             tiles_kernel,
             out_shape=(jax.ShapeDtypeStruct((devices // 2, own, rank), jnp.float32),) * 2,
-            in_specs=[HBM, HBM, HBM, VMEM, VMEM, VMEM, VMEM],
+            in_specs=[HBM, HBM, HBM, VMEM, VMEM, VMEM, VMEM, VMEM],
             out_specs=(VMEM, VMEM),
             scratch_shapes=[
                 pltpu.SMEM(plan_shape, jnp.int32),
@@ -311,8 +307,8 @@
             ]
             + [pltpu.VMEM((GROUP * TILE, rank), jnp.bfloat16)] * UNROLL
             + [pltpu.VMEM((TILE, GROUP * TILE), jnp.bfloat16)] * UNROLL,
-            compiler_params=pltpu.CompilerParams(vmem_limit_bytes=51 * MIB),
-        )(plan, tile_counts, mate_counts, first_counts, gathered, items, day_rows)
+            compiler_params=pltpu.CompilerParams(vmem_limit_bytes=50 * MIB),
+        )(plan, tile_counts, mate_counts, first_counts, gathered, items, across, day_rows)
         chip_sum = (kept + lax.ppermute(sent, "day", mates)).astype(jnp.bfloat16)
         extra = pl.pallas_call(
             functools.partial(sums_kernel, n_day // 2),

time: 40.8 us -> 40.4 us (level)
  Pallas kernels: 8.08 us -> 7.24 us
  waiting for transfers between devices: 5.28 us -> 5.81 us
    all_to_all x1, waiting for transfers between devices: 3.38 us -> 3.92 us  [per_device(): lax.all_to_all(spread, axes, 0, 0, tiled=True).reshape(devices * own, rank)]
    pallas_call x1, Pallas kernels: 2.72 us -> 2.18 us  [per_device(): pl.pallas_call(functools.partial(plan_kernel, blocks), out_shape=(jax.Sha...]
  transfers between devices with their start and end apart: 6 -> 6, of which waited for: 3 -> 3; matrix products, arithmetic and copies ran while one was open for 4% -> 4% of each run, Pallas kernels for 7% -> 6%
where the time goes in v2:
time: 40.4 us; the launch traced here: 39.7 us
  blocking collectives  13.6 us (34%)
  starting transfers between devices  8.31 us (21%)
  Pallas kernels  7.24 us (18%)
  waiting for transfers between devices  5.81 us (14%)
  local copies, waits for them, and re-layouts  3.25 us (8%)
  other arithmetic  0.77 us (2%)
  between operations  0.72 us (2%)
    all_to_all x1, blocking collectives, per_device(): lax.all_to_all(jnp.concatenate([chip_sum, sums], axis=2), axes, 0, 0, axi...  13.6 us
    all_to_all x1, starting transfers between devices, per_device(): lax.all_to_all(spread, axes, 0, 0, tiled=True).reshape(devices * own, rank)  6.96 us
    pallas_call x1, Pallas kernels, per_device(): pl.pallas_call(tiles_kernel, out_shape=(jax.ShapeDtypeStruct((devices //...  4.31 us
    all_to_all x1, waiting for transfers between devices, per_device(): lax.all_to_all(spread, axes, 0, 0, tiled=True).reshape(devices * own, rank)  3.92 us
    unnamed x8, local copies, waits for them, and re-layouts  2.52 us
    pallas_call x1, Pallas kernels, per_device(): pl.pallas_call(functools.partial(plan_kernel, blocks), out_shape=(jax.Sha...  2.18 us
    ppermute x1, waiting for transfers between devices, per_device(): chip_sum = (kept + lax.ppermute(sent, 'day', mates)).astype(jnp.bfloat16)  1.41 us
    ppermute x4, starting transfers between devices, per_device(): lax.ppermute(x, 'day', mates)  1.28 us
  transfers between devices with their start and end apart: 6, of which 3 were waited for; matrix products, arithmetic and copies ran while one was open for 4% of the time, Pallas kernels for 6%

profile of v2, /device:TPU:0, one launch (start us, length us, event | category | flops | bytes accessed | tf_op | source)
XLA Modules:
  0.0 39.7 jit_solution(5046859752042330696)
XLA Ops:
  0.0 0.5 %collective-permute-start.3 = (bf16[128,128,128]{2,1,0:T(8,128)(2,1)}, bf16[128,128,128]{2,1,0:T(8,128)(2,1)}, u32[]{:S(2)}, u32[]{:S(2)}) collective-permute-start(bf16[128,128,128]{2,1,0:T(8,128)(2,1)} %counts_far.3), channel_id=1, source_target_pairs={{0,1},{1,0},{2,3},{3,2},{4,5},{5,4},{6,7},{7,6},{8,9},{9,8},{10,11... | collective-permute-start | bytes 12582920 | tf_op jit(solution)/shard_map/ppermute | solution.py:271
  0.5 0.7 %convert_element_type.6 = bf16[8,512]{1,0:T(8,128)(2,1)S(1)} convert(f32[8,512]{1,0:T(8,128)} %user_factors.1) | non-fusion elementwise | flops 4096 | bytes 24576 | tf_op jit(solution)/shard_map/convert_element_type | solution.py:274
  1.2 0.7 %broadcast_in_dim.4 = bf16[32,8,512]{2,1,0:T(8,128)(2,1)} broadcast(bf16[8,512]{1,0:T(8,128)(2,1)S(1)} %convert_element_type.6), dimensions={1,2} | broadcast | bytes 270336 | tf_op jit(solution)/shard_map/broadcast_in_dim | solution.py:274
  1.9 7.0 %all-to-all-start = ((bf16[32,8,512]{2,1,0:T(8,128)(2,1)}), bf16[32,8,512]{2,1,0:T(8,128)(2,1)S(1)}, u32[]{:S(2)}, u32[]{:S(2)}) async-start(bf16[32,8,512]{2,1,0:T(8,128)(2,1)} %broadcast_in_dim.4), calls=%async_computation | async-start | bytes 524288 | tf_op jit(solution)/shard_map/all_to_all | solution.py:275
  8.9 0.3 collective-permute-start.2
  9.2 0.3 collective-permute-start.1
  9.4 0.3 collective-permute-start
  10.3 0.5 %collective-permute-done.mate_live = s32[1]{0:T(128)} collective-permute-done((s32[1]{0:T(128)}, s32[1]{0:T(128)}, u32[]{:S(2)}, u32[]{:S(2)}) %collective-permute-start) | collective-permute-done | bytes 36 | tf_op jit(solution)/shard_map/ppermute | solution.py:271
  10.8 0.0 collective-permute-done.1.mate_index
  10.8 0.0 collective-permute-done.2.mate_days
  10.8 0.0 copy-start
  10.8 1.0 %copy-done = bf16[512,512]{1,0:T(8,128)(2,1)S(1)} copy-done((bf16[512,512]{1,0:T(8,128)(2,1)S(1)}, bf16[512,512]{1,0:T(8,128)(2,1)}, u32[]{:S(2)}) %copy-start) | copy-done | bytes 524312
  11.9 0.0 copy-start.2
  11.9 0.8 %copy-done.2 = bf16[46,512]{1,0:T(8,128)(2,1)S(1)} copy-done((bf16[46,512]{1,0:T(8,128)(2,1)S(1)}, bf16[46,512]{1,0:T(8,128)(2,1)}, u32[]{:S(2)}) %copy-start.2) | copy-done | bytes 47128
  12.7 0.0 copy-start.3
  12.7 0.7 %copy-done.3 = s32[3,128]{1,0:T(4,128)S(1)} copy-done((s32[3,128]{1,0:T(4,128)S(1)}, s32[3,128]{1,0:T(4,128)}, u32[]{:S(2)}) %copy-start.3) | copy-done | bytes 1560
  13.4 2.2 %shard_map.64 = (s32[3,128]{1,0:T(4,128)S(1)}, bf16[512,512]{1,0:T(8,128)(2,1)S(1)}, bf16[512,512]{1,0:T(8,128)(2,1)S(1)}, f32[96,512]{1,0:T(8,128)S(1)}, bf16[48,128,128]{2,1,0:T(8,128)(2,1)S(1)}) custom-call(s32[1]{0:T(128)S(6)} %copy.7.live, s32[1]{0:T(128)} %collective-permute-done.mate_live, s32[3,128]{1,0:T(4,128)S(1)} %copy-done.3, ...), custom_call_target="tpu_custom_call" | custom-call | tf_op jit(solution)/shard_map/pallas_call | solution.py:276
  15.5 3.9 %all-to-all-done = bf16[32,8,512]{2,1,0:T(8,128)(2,1)S(1)} async-done(((bf16[32,8,512]{2,1,0:T(8,128)(2,1)}), bf16[32,8,512]{2,1,0:T(8,128)(2,1)S(1)}, u32[]{:S(2)}, u32[]{:S(2)}) %all-to-all-start) | async-done | bytes 262176 | tf_op jit(solution)/shard_map/all_to_all | solution.py:275
  19.5 0.0 collective-permute-done.3.mate_counts_far
  19.5 0.0 copy-start.1
  19.5 4.3 %shard_map.65 = (f32[16,8,512]{2,1,0:T(8,128)S(1)}, f32[16,8,512]{2,1,0:T(8,128)S(1)}) custom-call(s32[3,128]{1,0:T(4,128)S(1)} %get-tuple-element.12.plan_far, bf16[128,128,128]{2,1,0:T(8,128)(2,1)} %counts_far.3, bf16[128,128,128]{2,1,0:T(8,128)(2,1)} %collective-permute-done.3.mate_counts_far, bf16[48,128,128]{2,1,0:T(8,128)(2,1)S(1)} %get-tuple-element.13.first_counts, ...), custom_call_target="tpu_custom_call" | custom-call | tf_op jit(solution)/shard_map/pallas_call | solution.py:296
  23.8 0.1 collective-permute-start.4
  23.9 0.1 shard_map.66
  24.0 1.4 %collective-permute-done.4 = f32[16,8,512]{2,1,0:T(8,128)S(1)} collective-permute-done((f32[16,8,512]{2,1,0:T(8,128)S(1)}, f32[16,8,512]{2,1,0:T(8,128)S(1)}, u32[]{:S(2)}, u32[]{:S(2)}) %collective-permute-start.4) | collective-permute-done | bytes 262176 | tf_op jit(solution)/shard_map/ppermute | solution.py:312
  25.5 13.6 %all_to_all.10.received = bf16[16,8,640]{2,1,0:T(8,128)(2,1)S(1)} all-to-all(bf16[16,8,640]{2,1,0:T(8,128)(2,1)S(1)} %pad_maximum_fusion), channel_id=1, replica_groups={{0,2,4,6,8,10,12,14,16,18,20,22,24,26,28,30},{1,3,5,7,9,11,13,15,17,19,..., dimensions={0} | all-to-all | bytes 327680 | tf_op jit(solution)/shard_map/all_to_all | solution.py:321
  39.0 0.0 copy-done.1
  39.0 0.6 %shard_map.67 = f32[8,512]{1,0:T(8,128)} custom-call(bf16[16,8,640]{2,1,0:T(8,128)(2,1)S(1)} %all_to_all.10.received, f32[8,512]{1,0:T(8,128)S(1)} %copy-done.1), custom_call_target="tpu_custom_call" | custom-call | tf_op jit(solution)/shard_map/pallas_call | solution.py:329
  (3 shorter events, 0.1 us)
Async XLA Ops:
  0.0 19.5 %collective-permute-start.3 = (bf16[128,128,128]{2,1,0:T(8,128)(2,1)}, bf16[128,128,128]{2,1,0:T(8,128)(2,1)}, u32[]{:S(2)}, u32[]{:S(2)}) collective-permute-start(bf16[128,128,128]{2,1,0:T(8,128)(2,1)} %counts_far.3), channel_id=1, source_target_pairs={{0,1},{1,0},{2,3},{3,2},{4,5},{5,4},{6,7},{7,6},{8,9},{9,8},{10,11... | collective-permute-start | bytes 12582920 | tf_op jit(solution)/shard_map/ppermute | solution.py:271
  1.9 17.6 %all-to-all-start = ((bf16[32,8,512]{2,1,0:T(8,128)(2,1)}), bf16[32,8,512]{2,1,0:T(8,128)(2,1)S(1)}, u32[]{:S(2)}, u32[]{:S(2)}) async-start(bf16[32,8,512]{2,1,0:T(8,128)(2,1)} %broadcast_in_dim.4), calls=%async_computation | async-start | bytes 524288 | tf_op jit(solution)/shard_map/all_to_all | solution.py:275
  8.9 2.0 %collective-permute-start.2 = (bf16[46,512]{1,0:T(8,128)(2,1)}, bf16[46,512]{1,0:T(8,128)(2,1)S(1)}, u32[]{:S(2)}, u32[]{:S(2)}) collective-permute-start(bf16[46,512]{1,0:T(8,128)(2,1)} %days_far.1), channel_id=1, source_target_pairs={{0,1},{1,0},{2,3},{3,2},{4,5},{5,4},{6,7},{7,6},{8,9},{9,8},{10,11... | collective-permute-start | bytes 141320 | tf_op jit(solution)/shard_map/ppermute | solution.py:271
  9.2 1.6 %collective-permute-start.1 = (s32[3,128]{1,0:T(4,128)}, s32[3,128]{1,0:T(4,128)S(1)}, u32[]{:S(2)}, u32[]{:S(2)}) collective-permute-start(s32[3,128]{1,0:T(4,128)} %index.1), channel_id=1, source_target_pairs={{0,1},{1,0},{2,3},{3,2},{4,5},{5,4},{6,7},{7,6},{8,9},{9,8},{10,11... | collective-permute-start | bytes 4616 | tf_op jit(solution)/shard_map/ppermute | solution.py:271
  9.4 1.4 %collective-permute-start = (s32[1]{0:T(128)}, s32[1]{0:T(128)}, u32[]{:S(2)}, u32[]{:S(2)}) collective-permute-start(s32[1]{0:T(128)} %param.11), channel_id=1, source_target_pairs={{0,1},{1,0},{2,3},{3,2},{4,5},{5,4},{6,7},{7,6},{8,9},{9,8},{10,11... | collective-permute-start | bytes 20 | tf_op jit(solution)/shard_map/ppermute | solution.py:271
  10.8 1.0 %copy-start = (bf16[512,512]{1,0:T(8,128)(2,1)S(1)}, bf16[512,512]{1,0:T(8,128)(2,1)}, u32[]{:S(2)}) copy-start(bf16[512,512]{1,0:T(8,128)(2,1)} %items_far.1) | copy-start | bytes 1572868
  11.9 0.8 %copy-start.2 = (bf16[46,512]{1,0:T(8,128)(2,1)S(1)}, bf16[46,512]{1,0:T(8,128)(2,1)}, u32[]{:S(2)}) copy-start(bf16[46,512]{1,0:T(8,128)(2,1)} %days_far.1) | copy-start | bytes 141316
  12.7 0.7 %copy-start.3 = (s32[3,128]{1,0:T(4,128)S(1)}, s32[3,128]{1,0:T(4,128)}, u32[]{:S(2)}) copy-start(s32[3,128]{1,0:T(4,128)} %index.1) | copy-start | bytes 4612
  19.5 19.6 %copy-start.1 = (f32[8,512]{1,0:T(8,128)S(1)}, f32[8,512]{1,0:T(8,128)}, u32[]{:S(2)}) copy-start(f32[8,512]{1,0:T(8,128)} %user_factors.1) | copy-start | bytes 49156
  23.8 1.6 %collective-permute-start.4 = (f32[16,8,512]{2,1,0:T(8,128)S(1)}, f32[16,8,512]{2,1,0:T(8,128)S(1)}, u32[]{:S(2)}, u32[]{:S(2)}) collective-permute-start(f32[16,8,512]{2,1,0:T(8,128)S(1)} %get-tuple-element.18), channel_id=1, source_target_pairs={{0,1},{1,0},{2,3},{3,2},{4,5},{5,4},{6,7},{7,6},{8,9},{9,8},{10,11... | collective-permute-start | bytes 786440 | tf_op jit(solution)/shard_map/ppermute | solution.py:312

commit v3 on v2

--- a/solution.py
+++ b/solution.py
@@ -9,7 +9,8 @@
 
 TILE = 128
 GROUP = 4
-UNROLL = 4
+UNROLL = 5
+TAIL = 2
 CHUNK = 16
 LANES = 128
 NEEDS = 8
@@ -219,15 +220,20 @@
             add_terms(jnp.maximum(g - 1, 0), (i - 1) % UNROLL)
         return need
 
-    turns = (groups + UNROLL - 2) // UNROLL
+    turns = (groups + UNROLL - 1 - TAIL) // UNROLL
     ready = lax.fori_loop(0, turns, turn, jnp.int32(FIRST))
     lax.fori_loop(ready, all_parts, wait_part, 0)
-    add_terms(jnp.maximum(turns * UNROLL - 1, 0), UNROLL - 1)
-
-    @pl.when(groups > turns * UNROLL)
-    def _():
-        make_ratio(turns * UNROLL, 0)
-        add_terms(turns * UNROLL, 0)
+    first = turns * UNROLL
+    rest = groups - first
+
+    def tail(count):
+        for i in range(count):
+            make_ratio(first + i, i)
+            add_terms(jnp.maximum(first + i - 1, 0), (i - 1) % UNROLL)
+        add_terms(jnp.maximum(first + count - 1, 0), (count - 1) % UNROLL)
+
+    for count, chosen in ((0, rest <= 0), (1, rest == 1), (TAIL, rest > 1)):
+        pl.when(chosen)(functools.partial(tail, count))
 
     own = kept.shape[1]
     core = lax.axis_index("day") & 1

time: 40.4 us -> 40.2 us (level); the launches traced: 39.7 us -> 40.6 us
  blocking collectives: 13.6 us -> 14.6 us
    all_to_all x1, blocking collectives: 13.6 us -> 14.6 us  [per_device(): lax.all_to_all(jnp.concatenate([chip_sum, sums], axis=2), axes, 0, 0, axi...]
where the time goes in v3:
time: 40.2 us; the launch traced here: 40.6 us
  blocking collectives  14.6 us (36%)
  starting transfers between devices  8.31 us (21%)
  Pallas kernels  7.12 us (18%)
  waiting for transfers between devices  5.81 us (14%)
  local copies, waits for them, and re-layouts  3.25 us (8%)
  other arithmetic  0.77 us (2%)
  between operations  0.72 us (2%)
    all_to_all x1, blocking collectives, per_device(): lax.all_to_all(jnp.concatenate([chip_sum, sums], axis=2), axes, 0, 0, axi...  14.6 us
    all_to_all x1, starting transfers between devices, per_device(): lax.all_to_all(spread, axes, 0, 0, tiled=True).reshape(devices * own, rank)  6.96 us
    pallas_call x1, Pallas kernels, per_device(): pl.pallas_call(tiles_kernel, out_shape=(jax.ShapeDtypeStruct((devices //...  4.19 us
    all_to_all x1, waiting for transfers between devices, per_device(): lax.all_to_all(spread, axes, 0, 0, tiled=True).reshape(devices * own, rank)  3.92 us
    unnamed x8, local copies, waits for them, and re-layouts  2.52 us
    pallas_call x1, Pallas kernels, per_device(): pl.pallas_call(functools.partial(plan_kernel, blocks), out_shape=(jax.Sha...  2.18 us
    ppermute x1, waiting for transfers between devices, per_device(): chip_sum = (kept + lax.ppermute(sent, 'day', mates)).astype(jnp.bfloat16)  1.41 us
    ppermute x4, starting transfers between devices, per_device(): lax.ppermute(x, 'day', mates)  1.28 us
  transfers between devices with their start and end apart: 6, of which 3 were waited for; matrix products, arithmetic and copies ran while one was open for 4% of the time, Pallas kernels for 6%

profile of v3, /device:TPU:0, one launch (start us, length us, event | category | flops | bytes accessed | tf_op | source)
XLA Modules:
  0.0 40.6 jit_solution(14482068454107935432)
XLA Ops:
  0.0 0.5 %collective-permute-start.3 = (bf16[128,128,128]{2,1,0:T(8,128)(2,1)}, bf16[128,128,128]{2,1,0:T(8,128)(2,1)}, u32[]{:S(2)}, u32[]{:S(2)}) collective-permute-start(bf16[128,128,128]{2,1,0:T(8,128)(2,1)} %counts_far.3), channel_id=1, source_target_pairs={{0,1},{1,0},{2,3},{3,2},{4,5},{5,4},{6,7},{7,6},{8,9},{9,8},{10,11... | collective-permute-start | bytes 12582920 | tf_op jit(solution)/shard_map/ppermute | solution.py:277
  0.5 0.7 %convert_element_type.6 = bf16[8,512]{1,0:T(8,128)(2,1)S(1)} convert(f32[8,512]{1,0:T(8,128)} %user_factors.1) | non-fusion elementwise | flops 4096 | bytes 24576 | tf_op jit(solution)/shard_map/convert_element_type | solution.py:280
  1.2 0.7 %broadcast_in_dim.4 = bf16[32,8,512]{2,1,0:T(8,128)(2,1)} broadcast(bf16[8,512]{1,0:T(8,128)(2,1)S(1)} %convert_element_type.6), dimensions={1,2} | broadcast | bytes 270336 | tf_op jit(solution)/shard_map/broadcast_in_dim | solution.py:280
  1.9 7.0 %all-to-all-start = ((bf16[32,8,512]{2,1,0:T(8,128)(2,1)}), bf16[32,8,512]{2,1,0:T(8,128)(2,1)S(1)}, u32[]{:S(2)}, u32[]{:S(2)}) async-start(bf16[32,8,512]{2,1,0:T(8,128)(2,1)} %broadcast_in_dim.4), calls=%async_computation | async-start | bytes 524288 | tf_op jit(solution)/shard_map/all_to_all | solution.py:281
  8.9 0.3 collective-permute-start.2
  9.2 0.3 collective-permute-start.1
  9.4 0.3 collective-permute-start
  10.3 0.5 %collective-permute-done.mate_live = s32[1]{0:T(128)} collective-permute-done((s32[1]{0:T(128)}, s32[1]{0:T(128)}, u32[]{:S(2)}, u32[]{:S(2)}) %collective-permute-start) | collective-permute-done | bytes 36 | tf_op jit(solution)/shard_map/ppermute | solution.py:277
  10.8 0.0 collective-permute-done.1.mate_index
  10.8 0.0 collective-permute-done.2.mate_days
  10.8 0.0 copy-start
  10.8 1.0 %copy-done = bf16[512,512]{1,0:T(8,128)(2,1)S(1)} copy-done((bf16[512,512]{1,0:T(8,128)(2,1)S(1)}, bf16[512,512]{1,0:T(8,128)(2,1)}, u32[]{:S(2)}) %copy-start) | copy-done | bytes 524312
  11.9 0.0 copy-start.2
  11.9 0.8 %copy-done.2 = bf16[46,512]{1,0:T(8,128)(2,1)S(1)} copy-done((bf16[46,512]{1,0:T(8,128)(2,1)S(1)}, bf16[46,512]{1,0:T(8,128)(2,1)}, u32[]{:S(2)}) %copy-start.2) | copy-done | bytes 47128
  12.7 0.0 copy-start.3
  12.7 0.7 %copy-done.3 = s32[3,128]{1,0:T(4,128)S(1)} copy-done((s32[3,128]{1,0:T(4,128)S(1)}, s32[3,128]{1,0:T(4,128)}, u32[]{:S(2)}) %copy-start.3) | copy-done | bytes 1560
  13.4 2.2 %shard_map.64 = (s32[3,128]{1,0:T(4,128)S(1)}, bf16[512,512]{1,0:T(8,128)(2,1)S(1)}, bf16[512,512]{1,0:T(8,128)(2,1)S(1)}, f32[96,512]{1,0:T(8,128)S(1)}, bf16[48,128,128]{2,1,0:T(8,128)(2,1)S(1)}) custom-call(s32[1]{0:T(128)S(6)} %copy.7.live, s32[1]{0:T(128)} %collective-permute-done.mate_live, s32[3,128]{1,0:T(4,128)S(1)} %copy-done.3, ...), custom_call_target="tpu_custom_call" | custom-call | tf_op jit(solution)/shard_map/pallas_call | solution.py:282
  15.5 3.9 %all-to-all-done = bf16[32,8,512]{2,1,0:T(8,128)(2,1)S(1)} async-done(((bf16[32,8,512]{2,1,0:T(8,128)(2,1)}), bf16[32,8,512]{2,1,0:T(8,128)(2,1)S(1)}, u32[]{:S(2)}, u32[]{:S(2)}) %all-to-all-start) | async-done | bytes 262176 | tf_op jit(solution)/shard_map/all_to_all | solution.py:281
  19.5 0.0 collective-permute-done.3.mate_counts_far
  19.5 0.0 copy-start.1
  19.5 4.2 %shard_map.65 = (f32[16,8,512]{2,1,0:T(8,128)S(1)}, f32[16,8,512]{2,1,0:T(8,128)S(1)}) custom-call(s32[3,128]{1,0:T(4,128)S(1)} %get-tuple-element.12.plan_far, bf16[128,128,128]{2,1,0:T(8,128)(2,1)} %counts_far.3, bf16[128,128,128]{2,1,0:T(8,128)(2,1)} %collective-permute-done.3.mate_counts_far, bf16[48,128,128]{2,1,0:T(8,128)(2,1)S(1)} %get-tuple-element.13.first_counts, ...), custom_call_target="tpu_custom_call" | custom-call | tf_op jit(solution)/shard_map/pallas_call | solution.py:302
  23.7 0.1 collective-permute-start.4
  23.7 0.1 shard_map.66
  23.9 1.4 %collective-permute-done.4 = f32[16,8,512]{2,1,0:T(8,128)S(1)} collective-permute-done((f32[16,8,512]{2,1,0:T(8,128)S(1)}, f32[16,8,512]{2,1,0:T(8,128)S(1)}, u32[]{:S(2)}, u32[]{:S(2)}) %collective-permute-start.4) | collective-permute-done | bytes 262176 | tf_op jit(solution)/shard_map/ppermute | solution.py:318
  25.3 14.6 %all_to_all.10.received = bf16[16,8,640]{2,1,0:T(8,128)(2,1)S(1)} all-to-all(bf16[16,8,640]{2,1,0:T(8,128)(2,1)S(1)} %pad_maximum_fusion), channel_id=1, replica_groups={{0,2,4,6,8,10,12,14,16,18,20,22,24,26,28,30},{1,3,5,7,9,11,13,15,17,19,..., dimensions={0} | all-to-all | bytes 327680 | tf_op jit(solution)/shard_map/all_to_all | solution.py:327
  39.9 0.0 copy-done.1
  39.9 0.6 %shard_map.67 = f32[8,512]{1,0:T(8,128)} custom-call(bf16[16,8,640]{2,1,0:T(8,128)(2,1)S(1)} %all_to_all.10.received, f32[8,512]{1,0:T(8,128)S(1)} %copy-done.1), custom_call_target="tpu_custom_call" | custom-call | tf_op jit(solution)/shard_map/pallas_call | solution.py:335
  (3 shorter events, 0.1 us)
Async XLA Ops:
  0.0 19.5 %collective-permute-start.3 = (bf16[128,128,128]{2,1,0:T(8,128)(2,1)}, bf16[128,128,128]{2,1,0:T(8,128)(2,1)}, u32[]{:S(2)}, u32[]{:S(2)}) collective-permute-start(bf16[128,128,128]{2,1,0:T(8,128)(2,1)} %counts_far.3), channel_id=1, source_target_pairs={{0,1},{1,0},{2,3},{3,2},{4,5},{5,4},{6,7},{7,6},{8,9},{9,8},{10,11... | collective-permute-start | bytes 12582920 | tf_op jit(solution)/shard_map/ppermute | solution.py:277
  1.9 17.6 %all-to-all-start = ((bf16[32,8,512]{2,1,0:T(8,128)(2,1)}), bf16[32,8,512]{2,1,0:T(8,128)(2,1)S(1)}, u32[]{:S(2)}, u32[]{:S(2)}) async-start(bf16[32,8,512]{2,1,0:T(8,128)(2,1)} %broadcast_in_dim.4), calls=%async_computation | async-start | bytes 524288 | tf_op jit(solution)/shard_map/all_to_all | solution.py:281
  8.9 2.0 %collective-permute-start.2 = (bf16[46,512]{1,0:T(8,128)(2,1)}, bf16[46,512]{1,0:T(8,128)(2,1)S(1)}, u32[]{:S(2)}, u32[]{:S(2)}) collective-permute-start(bf16[46,512]{1,0:T(8,128)(2,1)} %days_far.1), channel_id=1, source_target_pairs={{0,1},{1,0},{2,3},{3,2},{4,5},{5,4},{6,7},{7,6},{8,9},{9,8},{10,11... | collective-permute-start | bytes 141320 | tf_op jit(solution)/shard_map/ppermute | solution.py:277
  9.2 1.6 %collective-permute-start.1 = (s32[3,128]{1,0:T(4,128)}, s32[3,128]{1,0:T(4,128)S(1)}, u32[]{:S(2)}, u32[]{:S(2)}) collective-permute-start(s32[3,128]{1,0:T(4,128)} %index.1), channel_id=1, source_target_pairs={{0,1},{1,0},{2,3},{3,2},{4,5},{5,4},{6,7},{7,6},{8,9},{9,8},{10,11... | collective-permute-start | bytes 4616 | tf_op jit(solution)/shard_map/ppermute | solution.py:277
  9.4 1.4 %collective-permute-start = (s32[1]{0:T(128)}, s32[1]{0:T(128)}, u32[]{:S(2)}, u32[]{:S(2)}) collective-permute-start(s32[1]{0:T(128)} %param.11), channel_id=1, source_target_pairs={{0,1},{1,0},{2,3},{3,2},{4,5},{5,4},{6,7},{7,6},{8,9},{9,8},{10,11... | collective-permute-start | bytes 20 | tf_op jit(solution)/shard_map/ppermute | solution.py:277
  10.8 1.0 %copy-start = (bf16[512,512]{1,0:T(8,128)(2,1)S(1)}, bf16[512,512]{1,0:T(8,128)(2,1)}, u32[]{:S(2)}) copy-start(bf16[512,512]{1,0:T(8,128)(2,1)} %items_far.1) | copy-start | bytes 1572868
  11.9 0.8 %copy-start.2 = (bf16[46,512]{1,0:T(8,128)(2,1)S(1)}, bf16[46,512]{1,0:T(8,128)(2,1)}, u32[]{:S(2)}) copy-start(bf16[46,512]{1,0:T(8,128)(2,1)} %days_far.1) | copy-start | bytes 141316
  12.7 0.7 %copy-start.3 = (s32[3,128]{1,0:T(4,128)S(1)}, s32[3,128]{1,0:T(4,128)}, u32[]{:S(2)}) copy-start(s32[3,128]{1,0:T(4,128)} %index.1) | copy-start | bytes 4612
  19.5 20.5 %copy-start.1 = (f32[8,512]{1,0:T(8,128)S(1)}, f32[8,512]{1,0:T(8,128)}, u32[]{:S(2)}) copy-start(f32[8,512]{1,0:T(8,128)} %user_factors.1) | copy-start | bytes 49156
  23.7 1.6 %collective-permute-start.4 = (f32[16,8,512]{2,1,0:T(8,128)S(1)}, f32[16,8,512]{2,1,0:T(8,128)S(1)}, u32[]{:S(2)}, u32[]{:S(2)}) collective-permute-start(f32[16,8,512]{2,1,0:T(8,128)S(1)} %get-tuple-element.18), channel_id=1, source_target_pairs={{0,1},{1,0},{2,3},{3,2},{4,5},{5,4},{6,7},{7,6},{8,9},{9,8},{10,11... | collective-permute-start | bytes 786440 | tf_op jit(solution)/shard_map/ppermute | solution.py:318

commit v4 on v3

--- a/solution.py
+++ b/solution.py
@@ -9,8 +9,8 @@
 
 TILE = 128
 GROUP = 4
-UNROLL = 5
-TAIL = 2
+UNROLL = 4
+TAIL = 3
 CHUNK = 16
 LANES = 128
 NEEDS = 8
@@ -232,7 +232,8 @@
             add_terms(jnp.maximum(first + i - 1, 0), (i - 1) % UNROLL)
         add_terms(jnp.maximum(first + count - 1, 0), (count - 1) % UNROLL)
 
-    for count, chosen in ((0, rest <= 0), (1, rest == 1), (TAIL, rest > 1)):
+    for count in range(TAIL + 1):
+        chosen = rest <= 0 if count == 0 else rest == count
         pl.when(chosen)(functools.partial(tail, count))
 
     own = kept.shape[1]

time: 40.2 us -> 40.5 us (level); the launches traced: 40.6 us -> 40.4 us
  Pallas kernels: 7.12 us -> 6.68 us
    pallas_call x1, Pallas kernels: 4.19 us -> 3.75 us  [per_device(): pl.pallas_call(tiles_kernel, out_shape=(jax.ShapeDtypeStruct((devices //...]
where the time goes in v4:
time: 40.5 us; the launch traced here: 40.4 us
  blocking collectives  14.9 us (37%)
  starting transfers between devices  8.34 us (21%)
  Pallas kernels  6.68 us (16%)
  waiting for transfers between devices  5.79 us (14%)
  local copies, waits for them, and re-layouts  3.25 us (8%)
  other arithmetic  0.77 us (2%)
  between operations  0.71 us (2%)
    all_to_all x1, blocking collectives, per_device(): lax.all_to_all(jnp.concatenate([chip_sum, sums], axis=2), axes, 0, 0, axi...  14.9 us
    all_to_all x1, starting transfers between devices, per_device(): lax.all_to_all(spread, axes, 0, 0, tiled=True).reshape(devices * own, rank)  6.96 us
    all_to_all x1, waiting for transfers between devices, per_device(): lax.all_to_all(spread, axes, 0, 0, tiled=True).reshape(devices * own, rank)  3.92 us
    pallas_call x1, Pallas kernels, per_device(): pl.pallas_call(tiles_kernel, out_shape=(jax.ShapeDtypeStruct((devices //...  3.75 us
    unnamed x8, local copies, waits for them, and re-layouts  2.52 us
    pallas_call x1, Pallas kernels, per_device(): pl.pallas_call(functools.partial(plan_kernel, blocks), out_shape=(jax.Sha...  2.18 us
    ppermute x1, waiting for transfers between devices, per_device(): chip_sum = (kept + lax.ppermute(sent, 'day', mates)).astype(jnp.bfloat16)  1.39 us
    ppermute x4, starting transfers between devices, per_device(): lax.ppermute(x, 'day', mates)  1.28 us
  transfers between devices with their start and end apart: 6, of which 3 were waited for; matrix products, arithmetic and copies ran while one was open for 4% of the time, Pallas kernels for 6%

profile of v4, /device:TPU:0, one launch (start us, length us, event | category | flops | bytes accessed | tf_op | source)
XLA Modules:
  0.0 40.4 jit_solution(9826680338195383050)
XLA Ops:
  0.0 0.5 %collective-permute-start.3 = (bf16[128,128,128]{2,1,0:T(8,128)(2,1)}, bf16[128,128,128]{2,1,0:T(8,128)(2,1)}, u32[]{:S(2)}, u32[]{:S(2)}) collective-permute-start(bf16[128,128,128]{2,1,0:T(8,128)(2,1)} %counts_far.3), channel_id=1, source_target_pairs={{0,1},{1,0},{2,3},{3,2},{4,5},{5,4},{6,7},{7,6},{8,9},{9,8},{10,11... | collective-permute-start | bytes 12582920 | tf_op jit(solution)/shard_map/ppermute | solution.py:278
  0.5 0.7 %convert_element_type.6 = bf16[8,512]{1,0:T(8,128)(2,1)S(1)} convert(f32[8,512]{1,0:T(8,128)} %user_factors.1) | non-fusion elementwise | flops 4096 | bytes 24576 | tf_op jit(solution)/shard_map/convert_element_type | solution.py:281
  1.2 0.7 %broadcast_in_dim.4 = bf16[32,8,512]{2,1,0:T(8,128)(2,1)} broadcast(bf16[8,512]{1,0:T(8,128)(2,1)S(1)} %convert_element_type.6), dimensions={1,2} | broadcast | bytes 270336 | tf_op jit(solution)/shard_map/broadcast_in_dim | solution.py:281
  1.9 7.0 %all-to-all-start = ((bf16[32,8,512]{2,1,0:T(8,128)(2,1)}), bf16[32,8,512]{2,1,0:T(8,128)(2,1)S(1)}, u32[]{:S(2)}, u32[]{:S(2)}) async-start(bf16[32,8,512]{2,1,0:T(8,128)(2,1)} %broadcast_in_dim.4), calls=%async_computation | async-start | bytes 524288 | tf_op jit(solution)/shard_map/all_to_all | solution.py:282
  8.9 0.3 collective-permute-start.2
  9.2 0.3 collective-permute-start.1
  9.4 0.3 collective-permute-start
  10.3 0.5 %collective-permute-done.mate_live = s32[1]{0:T(128)} collective-permute-done((s32[1]{0:T(128)}, s32[1]{0:T(128)}, u32[]{:S(2)}, u32[]{:S(2)}) %collective-permute-start) | collective-permute-done | bytes 36 | tf_op jit(solution)/shard_map/ppermute | solution.py:278
  10.8 0.0 collective-permute-done.1.mate_index
  10.8 0.0 collective-permute-done.2.mate_days
  10.8 0.0 copy-start
  10.8 1.0 %copy-done = bf16[512,512]{1,0:T(8,128)(2,1)S(1)} copy-done((bf16[512,512]{1,0:T(8,128)(2,1)S(1)}, bf16[512,512]{1,0:T(8,128)(2,1)}, u32[]{:S(2)}) %copy-start) | copy-done | bytes 524312
  11.9 0.0 copy-start.2
  11.9 0.8 %copy-done.2 = bf16[46,512]{1,0:T(8,128)(2,1)S(1)} copy-done((bf16[46,512]{1,0:T(8,128)(2,1)S(1)}, bf16[46,512]{1,0:T(8,128)(2,1)}, u32[]{:S(2)}) %copy-start.2) | copy-done | bytes 47128
  12.7 0.0 copy-start.3
  12.7 0.7 %copy-done.3 = s32[3,128]{1,0:T(4,128)S(1)} copy-done((s32[3,128]{1,0:T(4,128)S(1)}, s32[3,128]{1,0:T(4,128)}, u32[]{:S(2)}) %copy-start.3) | copy-done | bytes 1560
  13.4 2.2 %shard_map.64 = (s32[3,128]{1,0:T(4,128)S(1)}, bf16[512,512]{1,0:T(8,128)(2,1)S(1)}, bf16[512,512]{1,0:T(8,128)(2,1)S(1)}, f32[96,512]{1,0:T(8,128)S(1)}, bf16[48,128,128]{2,1,0:T(8,128)(2,1)S(1)}) custom-call(s32[1]{0:T(128)S(6)} %copy.7.live, s32[1]{0:T(128)} %collective-permute-done.mate_live, s32[3,128]{1,0:T(4,128)S(1)} %copy-done.3, ...), custom_call_target="tpu_custom_call" | custom-call | tf_op jit(solution)/shard_map/pallas_call | solution.py:283
  15.5 3.9 %all-to-all-done = bf16[32,8,512]{2,1,0:T(8,128)(2,1)S(1)} async-done(((bf16[32,8,512]{2,1,0:T(8,128)(2,1)}), bf16[32,8,512]{2,1,0:T(8,128)(2,1)S(1)}, u32[]{:S(2)}, u32[]{:S(2)}) %all-to-all-start) | async-done | bytes 262176 | tf_op jit(solution)/shard_map/all_to_all | solution.py:282
  19.5 0.0 collective-permute-done.3.mate_counts_far
  19.5 0.0 copy-start.1
  19.5 3.7 %shard_map.65 = (f32[16,8,512]{2,1,0:T(8,128)S(1)}, f32[16,8,512]{2,1,0:T(8,128)S(1)}) custom-call(s32[3,128]{1,0:T(4,128)S(1)} %get-tuple-element.12.plan_far, bf16[128,128,128]{2,1,0:T(8,128)(2,1)} %counts_far.3, bf16[128,128,128]{2,1,0:T(8,128)(2,1)} %collective-permute-done.3.mate_counts_far, bf16[48,128,128]{2,1,0:T(8,128)(2,1)S(1)} %get-tuple-element.13.first_counts, ...), custom_call_target="tpu_custom_call" | custom-call | tf_op jit(solution)/shard_map/pallas_call | solution.py:303
  23.2 0.1 collective-permute-start.4
  23.3 0.1 shard_map.66
  23.4 1.4 %collective-permute-done.4 = f32[16,8,512]{2,1,0:T(8,128)S(1)} collective-permute-done((f32[16,8,512]{2,1,0:T(8,128)S(1)}, f32[16,8,512]{2,1,0:T(8,128)S(1)}, u32[]{:S(2)}, u32[]{:S(2)}) %collective-permute-start.4) | collective-permute-done | bytes 262176 | tf_op jit(solution)/shard_map/ppermute | solution.py:319
  24.9 14.9 %all_to_all.10.received = bf16[16,8,640]{2,1,0:T(8,128)(2,1)S(1)} all-to-all(bf16[16,8,640]{2,1,0:T(8,128)(2,1)S(1)} %pad_maximum_fusion), channel_id=1, replica_groups={{0,2,4,6,8,10,12,14,16,18,20,22,24,26,28,30},{1,3,5,7,9,11,13,15,17,19,..., dimensions={0} | all-to-all | bytes 327680 | tf_op jit(solution)/shard_map/all_to_all | solution.py:328
  39.8 0.0 copy-done.1
  39.8 0.6 %shard_map.67 = f32[8,512]{1,0:T(8,128)} custom-call(bf16[16,8,640]{2,1,0:T(8,128)(2,1)S(1)} %all_to_all.10.received, f32[8,512]{1,0:T(8,128)S(1)} %copy-done.1), custom_call_target="tpu_custom_call" | custom-call | tf_op jit(solution)/shard_map/pallas_call | solution.py:336
  (3 shorter events, 0.1 us)
Async XLA Ops:
  0.0 19.5 %collective-permute-start.3 = (bf16[128,128,128]{2,1,0:T(8,128)(2,1)}, bf16[128,128,128]{2,1,0:T(8,128)(2,1)}, u32[]{:S(2)}, u32[]{:S(2)}) collective-permute-start(bf16[128,128,128]{2,1,0:T(8,128)(2,1)} %counts_far.3), channel_id=1, source_target_pairs={{0,1},{1,0},{2,3},{3,2},{4,5},{5,4},{6,7},{7,6},{8,9},{9,8},{10,11... | collective-permute-start | bytes 12582920 | tf_op jit(solution)/shard_map/ppermute | solution.py:278
  1.9 17.6 %all-to-all-start = ((bf16[32,8,512]{2,1,0:T(8,128)(2,1)}), bf16[32,8,512]{2,1,0:T(8,128)(2,1)S(1)}, u32[]{:S(2)}, u32[]{:S(2)}) async-start(bf16[32,8,512]{2,1,0:T(8,128)(2,1)} %broadcast_in_dim.4), calls=%async_computation | async-start | bytes 524288 | tf_op jit(solution)/shard_map/all_to_all | solution.py:282
  8.9 2.0 %collective-permute-start.2 = (bf16[46,512]{1,0:T(8,128)(2,1)}, bf16[46,512]{1,0:T(8,128)(2,1)S(1)}, u32[]{:S(2)}, u32[]{:S(2)}) collective-permute-start(bf16[46,512]{1,0:T(8,128)(2,1)} %days_far.1), channel_id=1, source_target_pairs={{0,1},{1,0},{2,3},{3,2},{4,5},{5,4},{6,7},{7,6},{8,9},{9,8},{10,11... | collective-permute-start | bytes 141320 | tf_op jit(solution)/shard_map/ppermute | solution.py:278
  9.2 1.6 %collective-permute-start.1 = (s32[3,128]{1,0:T(4,128)}, s32[3,128]{1,0:T(4,128)S(1)}, u32[]{:S(2)}, u32[]{:S(2)}) collective-permute-start(s32[3,128]{1,0:T(4,128)} %index.1), channel_id=1, source_target_pairs={{0,1},{1,0},{2,3},{3,2},{4,5},{5,4},{6,7},{7,6},{8,9},{9,8},{10,11... | collective-permute-start | bytes 4616 | tf_op jit(solution)/shard_map/ppermute | solution.py:278
  9.4 1.4 %collective-permute-start = (s32[1]{0:T(128)}, s32[1]{0:T(128)}, u32[]{:S(2)}, u32[]{:S(2)}) collective-permute-start(s32[1]{0:T(128)} %param.11), channel_id=1, source_target_pairs={{0,1},{1,0},{2,3},{3,2},{4,5},{5,4},{6,7},{7,6},{8,9},{9,8},{10,11... | collective-permute-start | bytes 20 | tf_op jit(solution)/shard_map/ppermute | solution.py:278
  10.8 1.0 %copy-start = (bf16[512,512]{1,0:T(8,128)(2,1)S(1)}, bf16[512,512]{1,0:T(8,128)(2,1)}, u32[]{:S(2)}) copy-start(bf16[512,512]{1,0:T(8,128)(2,1)} %items_far.1) | copy-start | bytes 1572868
  11.9 0.8 %copy-start.2 = (bf16[46,512]{1,0:T(8,128)(2,1)S(1)}, bf16[46,512]{1,0:T(8,128)(2,1)}, u32[]{:S(2)}) copy-start(bf16[46,512]{1,0:T(8,128)(2,1)} %days_far.1) | copy-start | bytes 141316
  12.7 0.7 %copy-start.3 = (s32[3,128]{1,0:T(4,128)S(1)}, s32[3,128]{1,0:T(4,128)}, u32[]{:S(2)}) copy-start(s32[3,128]{1,0:T(4,128)} %index.1) | copy-start | bytes 4612
  19.5 20.3 %copy-start.1 = (f32[8,512]{1,0:T(8,128)S(1)}, f32[8,512]{1,0:T(8,128)}, u32[]{:S(2)}) copy-start(f32[8,512]{1,0:T(8,128)} %user_factors.1) | copy-start | bytes 49156
  23.2 1.6 %collective-permute-start.4 = (f32[16,8,512]{2,1,0:T(8,128)S(1)}, f32[16,8,512]{2,1,0:T(8,128)S(1)}, u32[]{:S(2)}, u32[]{:S(2)}) collective-permute-start(f32[16,8,512]{2,1,0:T(8,128)S(1)} %get-tuple-element.18), channel_id=1, source_target_pairs={{0,1},{1,0},{2,3},{3,2},{4,5},{5,4},{6,7},{7,6},{8,9},{9,8},{10,11... | collective-permute-start | bytes 786440 | tf_op jit(solution)/shard_map/ppermute | solution.py:319
